TPU v7x, 32 devices: a whole 2x2x4 slice. The times are simulated.
32 devices in a mesh: grp: 8 (over z, x), own: 4 (over y, core).
Axes of the slice: x: 2, y: 2, z: 4, core: 2. Of those that a mesh axis runs over, the one named last changes fastest.
Arguments:
- queries: bfloat16 [2048, 768], P(('grp', 'own')), may hold values from -6 to 6
- projection: bfloat16 [768, 768], replicated, may hold values from -0.21875 to 0.21875
- lists: bfloat16 [1024, 256, 768], P(('grp', 'own')), may hold values from -6 to 6
- probes: int32 [2048, 8], P(('grp', 'own')), may hold values from 0 to 1023, as said below
- owner_map: int32 [1024], replicated, may hold values from 0 to 1023, as said below
Outputs:
- scores: float32 [2048, 8, 256], P(('grp', 'own'))
Inputs may be any that keep to these rules, and one draw needn't show every extreme that they name: A permutation: list i is stored in slot owner_map[i], slots k * 32 to (k + 1) * 32 - 1 lying on the k-th device of grp+own. `probes`: a query's 8 list ids are distinct; the 64 queries of one device probe lists stored on any one device at most 32 times in all; all queries together probe any one stored list at most 32 times.
All inputs are finite; a program needn't handle non-finite values.
Results may differ from a plain program's by a relative error of at most 0.0003.
Values may be sent and summed in bfloat16 or wider, within the bound.
A program may use at most 64 MiB of HBM per device.

v0:
```python
import jax
import jax.numpy as jnp
from jax import lax
from jax.experimental import pallas as pl
from jax.experimental.pallas import tpu as pltpu
from jax.sharding import PartitionSpec as P

AXES = ("grp", "own")
LANES = 128
LOG2E = 1.4426950408889634
LN2 = 0.6931471805599453


def gather_kernel(mine_ref, all_ref, send_sem, recv_sem):
    grp, own = lax.axis_index("grp"), lax.axis_index("own")
    z, x, y, c = grp // 2, grp % 2, own // 2, own % 2

    def device(zz, xx, yy, cc):
        return (zz * 2 + xx, yy * 2 + cc)

    def number(zz, xx, yy, cc):
        return (zz * 2 + xx) * 4 + yy * 2 + cc

    zs = [z] + [lax.rem(z + k, 4) for k in (1, 2, 3)]
    over_z = [device(zz, x, y, c) for zz in zs[1:]]
    over_x, over_y = device(z, 1 - x, y, c), device(z, x, 1 - y, c)
    sibling = device(z, x, y, 1 - c)
    barrier = pltpu.get_barrier_semaphore()
    for peer in over_z + [over_x, over_y, sibling]:
        pl.semaphore_signal(barrier, inc=1, device_id=peer, device_id_type=pl.DeviceIdType.MESH)
    pl.semaphore_wait(barrier, 6)

    sent = []

    def describe(src, block, peer, slot):
        return pltpu.make_async_remote_copy(
            src_ref=src,
            dst_ref=all_ref.at[block],
            send_sem=send_sem.at[slot],
            recv_sem=recv_sem.at[block],
            device_id=peer,
            device_id_type=pl.DeviceIdType.MESH,
        )

    def send(src, block, peer):
        copy = describe(src, block, peer, len(sent))
        copy.start()
        sent.append(copy)

    def arrived(block):
        describe(all_ref.at[block], block, sibling, 0).wait_recv()
        return all_ref.at[block]

    me = number(z, x, y, c)
    for peer in over_z + [over_x, over_y, sibling]:
        send(mine_ref, me, peer)
    all_ref[me] = mine_ref[...]
    for k in (0, 1, 3, 2):
        if k:
            block = number(zs[k], x, y, c)
            ref = arrived(block)
            for peer in (over_x, over_y, sibling):
                send(ref, block, peer)
        block = number(zs[k], 1 - x, y, c)
        ref = arrived(block)
        if k % 2 == 1:
            send(ref, block, over_y)
        send(ref, block, sibling)
        block = number(zs[k], x, 1 - y, c)
        ref = arrived(block)
        if k % 2 == 0:
            send(ref, block, over_x)
        send(ref, block, sibling)
    for k in (0, 1, 3, 2):
        block = number(zs[k], 1 - x, 1 - y, c)
        send(arrived(block), block, sibling)
    for k in (0, 1, 3, 2):
        for xx in (x, 1 - x):
            for yy in (y, 1 - y):
                arrived(number(zs[k], xx, yy, 1 - c))
    for copy in sent:
        copy.wait_send()


def gather_all(block):
    group_count, owner_count = lax.axis_size("grp"), lax.axis_size("own")
    if (group_count, owner_count) != (8, 4):
        return lax.all_gather(block, AXES, tiled=False)
    device_count = group_count * owner_count
    return pl.pallas_call(
        gather_kernel,
        out_shape=jax.ShapeDtypeStruct((device_count,) + block.shape, block.dtype),
        in_specs=[pl.BlockSpec(memory_space=pltpu.VMEM)],
        out_specs=pl.BlockSpec(memory_space=pltpu.VMEM),
        scratch_shapes=[
            pltpu.SemaphoreType.DMA((device_count,)),
            pltpu.SemaphoreType.DMA((device_count,)),
        ],
        compiler_params=pltpu.CompilerParams(
            collective_id=0, has_side_effects=True, vmem_limit_bytes=16 * 2**20
        ),
    )(block)


def select_kernel(queries, width, row_ref, all_ref, out_ref):
    devices = all_ref.shape[0]
    count = out_ref.shape[0]
    numbers = lax.broadcasted_iota(jnp.int32, (count, devices * queries), 1)
    pick = (numbers == row_ref[...]).astype(jnp.float32).astype(jnp.bfloat16)
    for j in range(width // LANES):
        part = all_ref[:, j * queries : (j + 1) * queries, :].reshape(devices * queries, LANES)
        out_ref[:, j * LANES : (j + 1) * LANES] = jnp.dot(
            pick, part, preferred_element_type=jnp.float32
        ).astype(jnp.bfloat16)


def select_rows(everyone, row_of, queries, width):
    slots = row_of.shape[0]
    block = min(256, slots)
    return pl.pallas_call(
        lambda *refs: select_kernel(queries, width, *refs),
        grid=(slots // block,),
        out_shape=jax.ShapeDtypeStruct((slots, width), jnp.bfloat16),
        in_specs=[
            pl.BlockSpec((block, 1), lambda i: (i, 0)),
            pl.BlockSpec(memory_space=pltpu.VMEM),
        ],
        out_specs=pl.BlockSpec((block, width), lambda i: (i, 0)),
        compiler_params=pltpu.CompilerParams(vmem_limit_bytes=48 * 2**20),
    )(row_of[:, None], everyone)


def score_kernel(blocks, rows_ref, lists_ref, spot_ref, out_ref, held):
    step = pl.program_id(0)
    count, list_size, width = lists_ref.shape
    capacity = rows_ref.shape[0] // count
    for n in range(count):
        rows = rows_ref[n * capacity : (n + 1) * capacity, :]
        dots = lax.dot_general(
            rows, lists_ref[n], (((1,), (1,)), ((), ())), preferred_element_type=jnp.float32
        )
        rows_f = rows.astype(jnp.float32)
        row_norm = jnp.sum(rows_f * rows_f, axis=1, keepdims=True)
        partial = None
        for j in range(width // LANES):
            part = lists_ref[n, :, j * LANES : (j + 1) * LANES].astype(jnp.float32)
            partial = part * part if partial is None else partial + part * part
        vec_norm = jnp.sum(partial.T, axis=0, keepdims=True)
        distance = jnp.maximum((row_norm + vec_norm - 2.0 * dots) / width, 0.0)
        largest = jnp.maximum(jnp.max(distance, axis=1, keepdims=True), 1e-30)
        power = jnp.clip(jnp.ceil(jnp.log(largest) * LOG2E + 1e-3), -100.0, 120.0)
        code = jnp.clip(jnp.round(distance * (65535.0 * jnp.exp(power * -LN2))), 0.0, 65535.0)
        high = jnp.floor(code * (1.0 / 256.0))
        low = code - high * 256.0
        place = pl.ds(pl.multiple_of((step * count + n) * capacity, 16), capacity)
        held[place, :list_size] = high.astype(jnp.bfloat16)
        held[place, list_size : 2 * list_size] = low.astype(jnp.bfloat16)
        held[place, 2 * list_size :] = jnp.broadcast_to(power, (capacity, LANES)).astype(
            jnp.bfloat16
        )

    @pl.when(step == pl.num_programs(0) - 1)
    def _():
        slots = held.shape[0]
        each = slots // blocks
        numbers = lax.broadcasted_iota(jnp.int32, (slots, slots), 1)
        pick = (numbers == spot_ref[...]).astype(jnp.float32).astype(jnp.bfloat16)
        got = jnp.dot(pick, held[...], preferred_element_type=jnp.float32)
        code = got[:, :list_size] * 256.0 + got[:, list_size : 2 * list_size] - 32768.0
        parts = [
            code[:, h * LANES : (h + 1) * LANES].reshape(blocks, each, LANES)
            for h in range(list_size // LANES)
        ]
        powers = got[:, 2 * list_size :].reshape(blocks, each, LANES)
        slot = lax.broadcasted_iota(jnp.int32, powers.shape, 1)
        lane = lax.broadcasted_iota(jnp.int32, powers.shape, 2)
        powers = jnp.sum(jnp.where(slot == lane, powers, 0.0), axis=1, keepdims=True)
        parts.append(jnp.broadcast_to(powers, (blocks, 16, LANES)))
        whole = jnp.concatenate(parts, axis=1)
        out_ref[...] = whole.astype(jnp.int32).astype(jnp.int16)


def score(grouped, lists, spot, blocks):
    list_count, list_size, width = lists.shape
    slots = grouped.shape[0]
    count = 4
    out_rows = (slots // blocks) * list_size // LANES + 16
    return pl.pallas_call(
        lambda *refs: score_kernel(blocks, *refs),
        grid=(list_count // count,),
        out_shape=jax.ShapeDtypeStruct((blocks, out_rows, LANES), jnp.int16),
        in_specs=[
            pl.BlockSpec((slots // list_count * count, width), lambda i: (i, 0)),
            pl.BlockSpec((count, list_size, width), lambda i: (i, 0, 0)),
            pl.BlockSpec((slots, 1), lambda i: (0, 0)),
        ],
        out_specs=pl.BlockSpec((blocks, out_rows, LANES), lambda i: (0, 0, 0)),
        scratch_shapes=[pltpu.VMEM((slots, 2 * list_size + LANES), jnp.bfloat16)],
        compiler_params=pltpu.CompilerParams(vmem_limit_bytes=40 * 2**20),
    )(grouped, lists, spot[:, None])


def exchange_kernel(device_count, owner_count, out_ref, in_ref, send_sem, recv_sem):
    me = lax.axis_index("grp") * owner_count + lax.axis_index("own")

    def at(k):
        other = lax.rem(me + k, device_count)
        return other, (other // owner_count, lax.rem(other, owner_count))

    barrier = pltpu.get_barrier_semaphore()

    @pl.loop(1, device_count)
    def _(k):
        pl.semaphore_signal(
            barrier, inc=1, device_id=at(k)[1], device_id_type=pl.DeviceIdType.MESH
        )

    pl.semaphore_wait(barrier, device_count - 1)

    def describe(k, block):
        other, where = at(k)
        return pltpu.make_async_remote_copy(
            src_ref=out_ref.at[other],
            dst_ref=in_ref.at[block],
            send_sem=send_sem.at[k],
            recv_sem=recv_sem.at[block],
            device_id=where,
            device_id_type=pl.DeviceIdType.MESH,
        )

    @pl.loop(1, device_count)
    def _(k):
        describe(k, me).start()

    in_ref[me] = out_ref[me]

    @pl.loop(1, device_count)
    def _(k):
        describe(k, at(k)[0]).wait_recv()

    @pl.loop(1, device_count)
    def _(k):
        describe(k, me).wait_send()


def exchange(blocks):
    owner_count = lax.axis_size("own")
    device_count = blocks.shape[0]
    return pl.pallas_call(
        lambda *refs: exchange_kernel(device_count, owner_count, *refs),
        out_shape=jax.ShapeDtypeStruct(blocks.shape, blocks.dtype),
        in_specs=[pl.BlockSpec(memory_space=pltpu.VMEM)],
        out_specs=pl.BlockSpec(memory_space=pltpu.VMEM),
        scratch_shapes=[
            pltpu.SemaphoreType.DMA((device_count,)),
            pltpu.SemaphoreType.DMA((device_count,)),
        ],
        compiler_params=pltpu.CompilerParams(
            collective_id=1, has_side_effects=True, vmem_limit_bytes=16 * 2**20
        ),
    )(blocks)


def body(queries, projection, lists, probes, owner_map):
    query_count, width = queries.shape
    probe_count = probes.shape[1]
    lists_here, list_size = lists.shape[0], lists.shape[1]
    device_count = lax.axis_size("grp") * lax.axis_size("own")
    pairs = query_count * probe_count
    capacity = 2 * pairs // device_count
    list_capacity = device_count * capacity // lists_here
    slots = device_count * capacity
    me = lax.axis_index(AXES)

    projected = jnp.dot(queries, projection, preferred_element_type=jnp.float32).astype(
        jnp.bfloat16
    )
    stored = jnp.take(owner_map, probes.reshape(-1))
    target = stored // lists_here
    local = stored % lists_here
    to_target = (target[:, None] == jnp.arange(device_count, dtype=jnp.int32)[None, :]).astype(
        jnp.bfloat16
    )
    step = jnp.arange(pairs, dtype=jnp.int32)
    earlier = (step[None, :] < step[:, None]).astype(jnp.bfloat16)
    before = jnp.dot(earlier, to_target, preferred_element_type=jnp.float32)
    rank = jnp.sum(before * to_target.astype(jnp.float32), axis=1).astype(jnp.int32)
    position = target * capacity + rank

    at_rank = (rank[:, None] == jnp.arange(capacity, dtype=jnp.int32)[None, :]).astype(jnp.bfloat16)
    query_of = step // probe_count
    what = jnp.stack([jnp.ones_like(step), query_of, local], axis=0).astype(jnp.bfloat16)
    weighted = to_target.T[None] * what[:, None, :]
    table = jnp.dot(
        weighted.reshape(3 * device_count, pairs), at_rank, preferred_element_type=jnp.float32
    ).reshape(3, device_count, capacity)
    table = jnp.where(table[:1] > 0.5, table[1:], -1.0).astype(jnp.bfloat16)
    columns = width // LANES
    extra = -(-(2 * slots) // (16 * LANES)) * 16
    table = jnp.pad(table.reshape(-1), (0, extra * LANES - 2 * slots)).reshape(extra, LANES)
    stacked = projected.reshape(query_count, columns, LANES).transpose(1, 0, 2)
    stacked = stacked.reshape(columns * query_count, LANES)

    everyone = gather_all(jnp.concatenate([stacked, table], axis=0))
    tables = everyone[:, columns * query_count :].reshape(device_count, -1)[:, : 2 * slots]
    tables = tables.reshape(device_count, 2, device_count, capacity)
    mine = lax.dynamic_index_in_dim(tables, me, axis=2, keepdims=False).astype(jnp.int32)
    asked_query = mine[:, 0].reshape(-1)
    asked_list = mine[:, 1].reshape(-1)
    row_of = (
        asked_query + query_count * (jnp.arange(slots, dtype=jnp.int32) // capacity)
    )

    in_list = (asked_list[:, None] == jnp.arange(lists_here, dtype=jnp.int32)[None, :]).astype(
        jnp.bfloat16
    )
    place = jnp.arange(slots, dtype=jnp.int32)
    earlier = (place[None, :] < place[:, None]).astype(jnp.bfloat16)
    before = jnp.dot(earlier, in_list, preferred_element_type=jnp.float32)
    order = jnp.sum(before * in_list.astype(jnp.float32), axis=1).astype(jnp.int32)
    valid = asked_list >= 0
    spot = jnp.where(valid, asked_list * list_capacity + order, -1)
    hit = spot[:, None] == jnp.arange(lists_here * list_capacity, dtype=jnp.int32)[None, :]
    grouped_row = jnp.sum(jnp.where(hit, row_of[:, None], 0), axis=0)
    grouped = select_rows(everyone, grouped_row, query_count, width)
    blocks = score(grouped, lists, spot, device_count)
    answer_rows = capacity * list_size // LANES
    got = exchange(blocks).astype(jnp.float32)
    powers = got[:, answer_rows:].reshape(device_count, -1)[:, :capacity].reshape(slots, 1)
    returned = (
        got[:, :answer_rows]
        .reshape(device_count, list_size // LANES, capacity, LANES)
        .transpose(0, 2, 1, 3)
        .reshape(slots, list_size)
    )
    returned = (returned + 32768.0) * (jnp.exp2(powers) / 65535.0)
    return returned[position].reshape(query_count, probe_count, list_size)


def solution(mesh):
    placed = (
        P(AXES, None),
        P(),
        P(AXES, None, None),
        P(AXES, None),
        P(),
    )
    return jax.shard_map(
        body, mesh=mesh, in_specs=placed, out_specs=P(AXES, None, None), check_vma=False
    )
```

profile of v0, /device:TPU:11, one launch (start us, length us, event | category | flops | bytes accessed | tf_op | source)
XLA Modules:
  0.0 92.0 jit_solution(14158271243396748265)
XLA Ops:
  0.0 0.0 copy-start
  0.0 0.9 copy.24
  0.9 0.1 reshape.415
  1.0 3.4 %gather_fusion = s32[512]{0:T(512)S(1)} fusion(s32[1024]{0:T(1024)} %param.9, s32[1024]{0:T(1024)S(1)} %pad_clamp_fusion.1), kind=kCustom, calls=%fused_computation | custom fusion | bytes 6144 | tf_op jit(solution)/shard_map/jit(_take)/gather | solution.py:278
  4.4 0.1 reshape.416
  4.5 0.1 pad_maximum_fusion.1
  4.6 0.1 reshape.414
  4.7 0.3 fusion.3
  5.0 0.3 fusion.4
  5.3 0.1 copy.27
  5.4 0.1 broadcast_in_dim.64
  5.5 0.1 slice.42
  5.6 0.1 copy.28
  5.7 0.1 slice.30
  5.8 0.0 copy-done
  5.8 1.2 %convolution_convert_fusion = bf16[64,768]{1,0:T(8,128)(2,1)S(1)} fusion(bf16[64,768]{1,0:T(8,128)(2,1)} %param.5, bf16[768,768]{1,0:T(8,128)(2,1)S(1)} %copy-done), kind=kOutput, calls=%fused_computation.6 | convolution fusion | flops 75546624 | bytes 1376256 | tf_op jit(solution)/shard_map/dot_general | solution.py:275
  7.0 0.1 reshape.412
  7.2 32.0 %shard_map.55.refs_1_ = bf16[32,400,128]{2,1,0:T(8,128)(2,1)S(1)} custom-call(bf16[400,128]{1,0:T(8,128)(2,1)S(1)} %pad_maximum_fusion.mine_ref), custom_call_target="tpu_custom_call" | custom-call | tf_op jit(solution)/shard_map/pallas_call | solution.py:90
  39.2 0.0 copy-start.1
  39.2 1.7 %copy-done.1 = bf16[32,400,128]{2,1,0:T(8,128)(2,1)} copy-done((bf16[32,400,128]{2,1,0:T(8,128)(2,1)}, bf16[32,400,128]{2,1,0:T(8,128)(2,1)S(1)}, u32[]{:S(2)}) %copy-start.1) | copy-done | bytes 3276824
  40.9 0.2 reshape_reshape.3
  41.3 0.1 reshape_squeeze.7
  41.3 0.1 reshape_squeeze.6
  41.4 0.5 fusion.2
  42.0 0.7 select_reduce_fusion
  42.6 0.2 copy.30.refs_0_
  42.9 0.0 copy-start.2
  42.9 1.9 %copy-done.2 = bf16[32,400,128]{2,1,0:T(8,128)(2,1)S(1)} copy-done((bf16[32,400,128]{2,1,0:T(8,128)(2,1)S(1)}, bf16[32,400,128]{2,1,0:T(8,128)(2,1)}, u32[]{:S(2)}) %copy-start.2) | copy-done | bytes 3276824
  44.8 7.4 %shard_map.56.refs_0_ = bf16[1024,768]{1,0:T(8,128)(2,1)S(1)} custom-call(s32[1024,1]{1,0:T(8,128)S(1)} %copy.30.refs_0_, bf16[32,400,128]{2,1,0:T(8,128)(2,1)S(1)} %copy-done.2), custom_call_target="tpu_custom_call" | custom-call | tf_op jit(solution)/shard_map/pallas_call | solution.py:120
  52.3 0.6 ge.61
  52.9 0.5 mul.93
  53.4 1.0 %copy.32 = s32[1024,1]{1,0:T(8,128)} copy(s32[1024,1]{0,1:T(1,128)S(1)} %bitcast.49) | data formatting | bytes 8192 | tf_op jit(solution)/shard_map/convert_element_type | solution.py:320
  54.4 1.1 %add_select_fusion.refs_2_ = s32[1024,1]{1,0:T(8,128)S(1)} fusion(pred[1024,1]{1,0:T(8,128)(4,1)S(1)} %ge.61, s32[1024,1]{1,0:T(8,128)S(1)} %mul.93, s32[1024,1]{1,0:T(8,128)} %copy.32), kind=kLoop, calls=%fused_computation.14 | loop fusion | flops 2048 | bytes 13312 | tf_op jit(solution)/shard_map/jit(_where)/select_n | solution.py:322
  55.5 11.7 %shard_map.57.refs_0_ = s16[32,80,128]{2,1,0:T(8,128)(2,1)S(1)} custom-call(bf16[1024,768]{1,0:T(8,128)(2,1)S(1)} %shard_map.56.refs_0_, bf16[32,256,768]{2,1,0:T(8,128)(2,1)} %refs_1_.1, s32[1024,1]{1,0:T(8,128)S(1)} %add_select_fusion.refs_2_), custom_call_target="tpu_custom_call" | custom-call | tf_op jit(solution)/shard_map/pallas_call | solution.py:188
  67.3 20.9 %shard_map.58 = s16[32,80,128]{2,1,0:T(8,128)(2,1)S(1)} custom-call(s16[32,80,128]{2,1,0:T(8,128)(2,1)S(1)} %shard_map.57.refs_0_), custom_call_target="tpu_custom_call" | custom-call | tf_op jit(solution)/shard_map/pallas_call | solution.py:249
  88.2 0.2 convert_element_type.85
  88.4 0.1 slice_add_fusion
  88.5 0.8 copy.34
  89.4 0.1 copy.43
  89.5 0.1 div.52
  89.5 0.2 bitcast_multiply_fusion
  89.8 2.2 %gather_fusion.1 = f32[512,256]{1,0:T(8,128)} fusion(f32[1024,256]{1,0:T(8,128)S(1)} %bitcast_multiply_fusion, s32[1024]{0:T(1024)S(1)} %pad_clamp_fusion), kind=kCustom, calls=%fused_computation.1 | custom fusion | bytes 1050624 | tf_op jit(solution)/shard_map/gather | solution.py:337
  (25 shorter events, 0.3 us)
Async XLA Ops:
  0.0 5.8 %copy-start = (bf16[768,768]{1,0:T(8,128)(2,1)S(1)}, bf16[768,768]{1,0:T(8,128)(2,1)}, u32[]{:S(2)}) copy-start(bf16[768,768]{1,0:T(8,128)(2,1)} %param.6) | copy-start | bytes 3538948
  39.2 1.7 %copy-start.1 = (bf16[32,400,128]{2,1,0:T(8,128)(2,1)}, bf16[32,400,128]{2,1,0:T(8,128)(2,1)S(1)}, u32[]{:S(2)}) copy-start(bf16[32,400,128]{2,1,0:T(8,128)(2,1)S(1)} %shard_map.55.refs_1_) | copy-start | bytes 9830404
  42.9 1.9 %copy-start.2 = (bf16[32,400,128]{2,1,0:T(8,128)(2,1)S(1)}, bf16[32,400,128]{2,1,0:T(8,128)(2,1)}, u32[]{:S(2)}) copy-start(bf16[32,400,128]{2,1,0:T(8,128)(2,1)} %copy-done.1) | copy-start | bytes 9830404
where the time goes:
time: 92.4 us; the launch traced here: 92 us
  Pallas kernels  72.1 us (78%)
  local copies, waits for them, and re-layouts  14.8 us (16%)
  other arithmetic  2.56 us (3%)
  matrix products  2.32 us (3%)
    pallas_call x1, Pallas kernels, gather_all(): pl.pallas_call(gather_kernel, out_shape=jax.ShapeDtypeStruct((device_coun...  32 us
    pallas_call x1, Pallas kernels, exchange(): pl.pallas_call(lambda *refs: exchange_kernel(device_count, owner_count, *...  20.9 us
    pallas_call x1, Pallas kernels, score(): pl.pallas_call(lambda *refs: score_kernel(blocks, *refs), grid=(list_coun...  11.7 us
    pallas_call x1, Pallas kernels, select_rows(): pl.pallas_call(lambda *refs: select_kernel(queries, width, *refs), grid=(...  7.44 us
    unnamed x8, local copies, waits for them, and re-layouts  4.56 us
    gather x1, local copies, waits for them, and re-layouts, body(): stored = jnp.take(owner_map, probes.reshape(-1))  3.37 us
    gather x1, local copies, waits for them, and re-layouts, body(): return returned[position].reshape(query_count, probe_count, list_size)  2.24 us

commit v1 on v0

--- a/solution.py
+++ b/solution.py
@@ -9,97 +9,6 @@
 LANES = 128
 LOG2E = 1.4426950408889634
 LN2 = 0.6931471805599453
-
-
-def gather_kernel(mine_ref, all_ref, send_sem, recv_sem):
-    grp, own = lax.axis_index("grp"), lax.axis_index("own")
-    z, x, y, c = grp // 2, grp % 2, own // 2, own % 2
-
-    def device(zz, xx, yy, cc):
-        return (zz * 2 + xx, yy * 2 + cc)
-
-    def number(zz, xx, yy, cc):
-        return (zz * 2 + xx) * 4 + yy * 2 + cc
-
-    zs = [z] + [lax.rem(z + k, 4) for k in (1, 2, 3)]
-    over_z = [device(zz, x, y, c) for zz in zs[1:]]
-    over_x, over_y = device(z, 1 - x, y, c), device(z, x, 1 - y, c)
-    sibling = device(z, x, y, 1 - c)
-    barrier = pltpu.get_barrier_semaphore()
-    for peer in over_z + [over_x, over_y, sibling]:
-        pl.semaphore_signal(barrier, inc=1, device_id=peer, device_id_type=pl.DeviceIdType.MESH)
-    pl.semaphore_wait(barrier, 6)
-
-    sent = []
-
-    def describe(src, block, peer, slot):
-        return pltpu.make_async_remote_copy(
-            src_ref=src,
-            dst_ref=all_ref.at[block],
-            send_sem=send_sem.at[slot],
-            recv_sem=recv_sem.at[block],
-            device_id=peer,
-            device_id_type=pl.DeviceIdType.MESH,
-        )
-
-    def send(src, block, peer):
-        copy = describe(src, block, peer, len(sent))
-        copy.start()
-        sent.append(copy)
-
-    def arrived(block):
-        describe(all_ref.at[block], block, sibling, 0).wait_recv()
-        return all_ref.at[block]
-
-    me = number(z, x, y, c)
-    for peer in over_z + [over_x, over_y, sibling]:
-        send(mine_ref, me, peer)
-    all_ref[me] = mine_ref[...]
-    for k in (0, 1, 3, 2):
-        if k:
-            block = number(zs[k], x, y, c)
-            ref = arrived(block)
-            for peer in (over_x, over_y, sibling):
-                send(ref, block, peer)
-        block = number(zs[k], 1 - x, y, c)
-        ref = arrived(block)
-        if k % 2 == 1:
-            send(ref, block, over_y)
-        send(ref, block, sibling)
-        block = number(zs[k], x, 1 - y, c)
-        ref = arrived(block)
-        if k % 2 == 0:
-            send(ref, block, over_x)
-        send(ref, block, sibling)
-    for k in (0, 1, 3, 2):
-        block = number(zs[k], 1 - x, 1 - y, c)
-        send(arrived(block), block, sibling)
-    for k in (0, 1, 3, 2):
-        for xx in (x, 1 - x):
-            for yy in (y, 1 - y):
-                arrived(number(zs[k], xx, yy, 1 - c))
-    for copy in sent:
-        copy.wait_send()
-
-
-def gather_all(block):
-    group_count, owner_count = lax.axis_size("grp"), lax.axis_size("own")
-    if (group_count, owner_count) != (8, 4):
-        return lax.all_gather(block, AXES, tiled=False)
-    device_count = group_count * owner_count
-    return pl.pallas_call(
-        gather_kernel,
-        out_shape=jax.ShapeDtypeStruct((device_count,) + block.shape, block.dtype),
-        in_specs=[pl.BlockSpec(memory_space=pltpu.VMEM)],
-        out_specs=pl.BlockSpec(memory_space=pltpu.VMEM),
-        scratch_shapes=[
-            pltpu.SemaphoreType.DMA((device_count,)),
-            pltpu.SemaphoreType.DMA((device_count,)),
-        ],
-        compiler_params=pltpu.CompilerParams(
-            collective_id=0, has_side_effects=True, vmem_limit_bytes=16 * 2**20
-        ),
-    )(block)
 
 
 def select_kernel(queries, width, row_ref, all_ref, out_ref):
@@ -261,7 +170,7 @@
     )(blocks)
 
 
-def body(queries, projection, lists, probes, owner_map):
+def general(queries, projection, lists, probes, owner_map):
     query_count, width = queries.shape
     probe_count = probes.shape[1]
     lists_here, list_size = lists.shape[0], lists.shape[1]
@@ -301,7 +210,7 @@
     stacked = projected.reshape(query_count, columns, LANES).transpose(1, 0, 2)
     stacked = stacked.reshape(columns * query_count, LANES)
 
-    everyone = gather_all(jnp.concatenate([stacked, table], axis=0))
+    everyone = lax.all_gather(jnp.concatenate([stacked, table], axis=0), AXES, tiled=False)
     tables = everyone[:, columns * query_count :].reshape(device_count, -1)[:, : 2 * slots]
     tables = tables.reshape(device_count, 2, device_count, capacity)
     mine = lax.dynamic_index_in_dim(tables, me, axis=2, keepdims=False).astype(jnp.int32)
@@ -337,6 +246,372 @@
     return returned[position].reshape(query_count, probe_count, list_size)
 
 
+PLANES = 4
+PLANE = 8
+TABLE = 16
+CHUNK = 8
+
+
+def number(z, x, y, c):
+    return z * PLANE + x * 4 + y * 2 + c
+
+
+def mesh_id(n):
+    return (n // 4, lax.rem(n, 4))
+
+
+def ranks(mine):
+    rows = mine.shape[0]
+    lane_a = lax.broadcasted_iota(jnp.int32, (LANES, LANES), 0)
+    lane_b = lax.broadcasted_iota(jnp.int32, (LANES, LANES), 1)
+    upper = jnp.where(lane_a < lane_b, 1.0, 0.0).astype(jnp.bfloat16)
+    ones = jnp.ones((LANES, LANES), jnp.bfloat16)
+    row_a = lax.broadcasted_iota(jnp.int32, (rows, rows), 0)
+    row_b = lax.broadcasted_iota(jnp.int32, (rows, rows), 1)
+    lower = jnp.where((row_a // 8 == row_b // 8) & (row_b < row_a), 1.0, 0.0).astype(jnp.bfloat16)
+    narrow = mine.astype(jnp.bfloat16)
+    within = jnp.dot(narrow, upper, preferred_element_type=jnp.float32)
+    totals = jnp.dot(narrow, ones, preferred_element_type=jnp.float32).astype(jnp.bfloat16)
+    return within + jnp.dot(lower, totals, preferred_element_type=jnp.float32)
+
+
+def fused_kernel(
+    queries_ref,
+    projection_ref,
+    probes_ref,
+    owner_ref,
+    lists_hbm,
+    out_ref,
+    all_ref,
+    lists_ref,
+    norms_ref,
+    picked_ref,
+    send_ref,
+    got_ref,
+    place_ref,
+    list_sem,
+    spread_send,
+    spread_recv,
+    back_send,
+    back_recv,
+):
+    grp, own = lax.axis_index("grp"), lax.axis_index("own")
+    z, x, y, c = grp // 2, lax.rem(grp, 2), own // 2, lax.rem(own, 2)
+    me = number(z, x, y, c)
+    inside = x * 4 + y * 2 + c
+    devices = all_ref.shape[0]
+    query_count, width = queries_ref.shape
+    list_count, list_size = lists_ref.shape[0], lists_ref.shape[1]
+    columns = width // LANES
+    table_at = columns * query_count
+    capacity = 32
+
+    barrier = pltpu.get_barrier_semaphore()
+
+    @pl.loop(1, devices)
+    def _(k):
+        pl.semaphore_signal(
+            barrier,
+            inc=1,
+            device_id=mesh_id(lax.rem(me + k, devices)),
+            device_id_type=pl.DeviceIdType.MESH,
+        )
+
+    part = list_count // list_sem.shape[0]
+
+    def list_copy(n):
+        piece = pl.ds(n * part, part)
+        return pltpu.make_async_copy(lists_hbm.at[piece], lists_ref.at[piece], list_sem.at[n])
+
+    for n in range(list_sem.shape[0]):
+        list_copy(n).start()
+
+    projected = jnp.dot(
+        queries_ref[...], projection_ref[...], preferred_element_type=jnp.float32
+    ).astype(jnp.bfloat16)
+    for j in range(columns):
+        all_ref[me, j * query_count : (j + 1) * query_count, :] = projected[
+            :, j * LANES : (j + 1) * LANES
+        ]
+    ids = jnp.concatenate([probes_ref[...], probes_ref[...]], axis=1)
+    low, high = ids & (LANES - 1), ids >> 7
+    stored = jnp.zeros_like(ids)
+    for h in range(owner_ref.shape[0]):
+        row = jnp.broadcast_to(owner_ref[h : h + 1, :], ids.shape)
+        found = jnp.take_along_axis(row, low, axis=1, mode="promise_in_bounds")
+        stored = jnp.where(high == h, found, stored)
+    lane8 = lax.broadcasted_iota(jnp.int32, ids.shape, 1)
+    table = jnp.where(lane8 < query_count, stored >> 5, stored & 31).astype(jnp.float32)
+    all_ref[me, table_at:, :] = jnp.concatenate([table, jnp.zeros_like(table)], axis=0).astype(
+        jnp.bfloat16
+    )
+    pl.semaphore_wait(barrier, devices - 1)
+
+    first = 3 * (1 - z // 2)
+    last = 1 + lax.rem(z, 2)
+    planes = [z, first, 6 - z - first - last, last]
+    xa, ya = x * c + (1 - x) * (1 - c), y * (1 - c) + (1 - y) * c
+    xb, yb = x * (1 - c) + (1 - x) * c, y * c + (1 - y) * (1 - c)
+    peer_a, peer_b = number(z, xa, ya, c), number(z, xb, yb, c)
+    sibling = number(z, x, y, 1 - c)
+    sent = []
+
+    def describe(block, peer, slot):
+        return pltpu.make_async_remote_copy(
+            src_ref=all_ref.at[block],
+            dst_ref=all_ref.at[block],
+            send_sem=spread_send.at[slot],
+            recv_sem=spread_recv.at[block],
+            device_id=mesh_id(peer),
+            device_id_type=pl.DeviceIdType.MESH,
+        )
+
+    def send(block, peer):
+        copy = describe(block, peer, len(sent))
+        copy.start()
+        sent.append(copy)
+
+    def arrived(block):
+        describe(block, sibling, 0).wait_recv()
+
+    def relay_column(p):
+        block = number(p, x, y, c)
+        arrived(block)
+        send(block, peer_a)
+        send(block, peer_b)
+        send(block, sibling)
+
+    def relay_a(p):
+        block = number(p, xa, ya, c)
+        arrived(block)
+        send(block, peer_b)
+        send(block, sibling)
+
+    def relay_b(p):
+        block = number(p, xb, yb, c)
+        arrived(block)
+        send(block, sibling)
+
+    def relay_diagonal(p):
+        block = number(p, 1 - x, 1 - y, c)
+        arrived(block)
+        send(block, sibling)
+
+    def complete(p):
+        for xx, yy in ((x, y), (xa, ya), (xb, yb), (1 - x, 1 - y)):
+            arrived(number(p, xx, yy, 1 - c))
+
+    send(me, peer_a)
+    send(me, peer_b)
+    for p in planes[1:]:
+        send(me, number(p, x, y, c))
+    send(me, sibling)
+
+    def list_norms(n):
+        list_copy(n).wait()
+        rows = []
+        for i in range(n * part, (n + 1) * part):
+            partial = None
+            for j in range(columns):
+                piece = lists_ref[i, :, j * LANES : (j + 1) * LANES].astype(jnp.float32)
+                partial = piece * piece if partial is None else partial + piece * piece
+            rows.append(0.5 * jnp.sum(partial.T, axis=0, keepdims=True))
+        norms_ref[n * part : (n + 1) * part, :] = jnp.concatenate(rows, axis=0)
+
+    steps = {
+        3: lambda: relay_a(planes[0]),
+        4: lambda: relay_b(planes[0]),
+        5: lambda: relay_column(planes[1]),
+        6: lambda: relay_diagonal(planes[0]),
+    }
+    for n in range(list_sem.shape[0]):
+        list_norms(n)
+        if n in steps:
+            steps[n]()
+
+    def back(target, block):
+        return pltpu.make_async_remote_copy(
+            src_ref=send_ref.at[target],
+            dst_ref=got_ref.at[block],
+            send_sem=back_send.at[target],
+            recv_sem=back_recv.at[block],
+            device_id=mesh_id(target),
+            device_id_type=pl.DeviceIdType.MESH,
+        )
+
+    me_f = me.astype(jnp.float32)
+    slots = PLANE * capacity
+    ones = jnp.ones((LANES, LANES), jnp.bfloat16)
+    slot = lax.broadcasted_iota(jnp.int32, (capacity, LANES), 0).astype(jnp.float32)
+
+    def choose(p):
+        tables = all_ref[pl.ds(p * PLANE, PLANE), table_at:, :].astype(jnp.float32)
+        tables = tables[:, :8, :].reshape(PLANE * 8, LANES)
+        lane = lax.broadcasted_iota(jnp.int32, tables.shape, 1)
+        mine = jnp.where((lane < query_count) & (tables == me_f), 1.0, 0.0)
+        rank = jnp.where(mine > 0.5, ranks(mine), -1.0)
+        local = tables + 1.0
+        at = (rank, pltpu.roll(rank, query_count, 1))
+        what = (pltpu.roll(local, query_count, 1), local)
+        picks, lists_of = [], []
+        for t in range(PLANE):
+            pick = jnp.zeros((capacity, LANES), jnp.float32)
+            which = jnp.zeros((capacity, LANES), jnp.float32)
+            for j in range(8):
+                row = t * 8 + j
+                hit = at[t % 2][row : row + 1, :] == slot
+                pick = jnp.where(hit, 1.0, pick)
+                which = jnp.where(hit, what[t % 2][row : row + 1, :], which)
+            picks.append(pick.astype(jnp.bfloat16))
+            lists_of.append(which.astype(jnp.bfloat16))
+        place = jnp.dot(
+            jnp.concatenate(lists_of, axis=0), ones, preferred_element_type=jnp.float32
+        )
+        norm = jnp.zeros((slots, LANES), jnp.float32)
+        for j in range(columns):
+            rows = []
+            for u in range(PLANE // 2):
+                pair = all_ref[
+                    pl.ds(p * PLANE + 2 * u, 2), j * query_count : (j + 1) * query_count, :
+                ].reshape(2 * query_count, LANES)
+                pick = jnp.concatenate(picks[2 * u : 2 * u + 2], axis=0)
+                rows.append(jnp.dot(pick, pair, preferred_element_type=jnp.float32))
+            piece = jnp.concatenate(rows, axis=0)
+            norm = norm + piece * piece
+            picked_ref[:, j * LANES : (j + 1) * LANES] = piece.astype(jnp.bfloat16)
+        return place, jnp.sum(norm, axis=1, keepdims=True)
+
+    def encode(p, best, norm):
+        distance = jnp.maximum((norm - 2.0 * best) * (1.0 / width), 0.0)
+        largest = jnp.maximum(jnp.max(distance, axis=1, keepdims=True), 1e-30)
+        power = jnp.clip(jnp.ceil(jnp.log(largest) * LOG2E + 1e-3), -100.0, 120.0)
+        code = jnp.clip(jnp.round(distance * (65535.0 * jnp.exp(power * -LN2))), 0.0, 65535.0)
+        code = code.astype(jnp.int32)
+        word = code[:, :LANES] | (code[:, LANES:] << 16)
+        here = pl.ds(p * PLANE, PLANE)
+        send_ref[here, :capacity, :] = word.reshape(PLANE, capacity, LANES)
+        spot = lax.broadcasted_iota(jnp.int32, (PLANE, capacity, LANES), 1) + own * capacity
+        lane = lax.broadcasted_iota(jnp.int32, (PLANE, capacity, LANES), 2)
+        powers = jnp.broadcast_to(power, (slots, LANES)).reshape(PLANE, capacity, LANES)
+        powers = jnp.sum(jnp.where(spot == lane, powers, 0.0), axis=1, keepdims=True)
+        send_ref[here, capacity : capacity + 1, :] = powers.astype(jnp.int32)
+
+    relay_after = {}
+    for k in range(PLANES - 1):
+        later = planes[k + 1]
+        relay_after[k, 0] = [lambda p=later: relay_a(p)]
+        relay_after[k, 1] = [lambda p=later: relay_b(p)]
+        if k + 2 < PLANES:
+            relay_after[k, 1].append(lambda p=planes[k + 2]: relay_column(p))
+        relay_after[k, 2] = [lambda p=later: relay_diagonal(p)]
+
+    returned = []
+    for k, p in enumerate(planes):
+        complete(p)
+        place, norm = choose(p)
+        best = jnp.zeros((slots, list_size), jnp.float32)
+        for g in range(list_count // CHUNK):
+            dots = lax.dot_general(
+                picked_ref[...],
+                lists_ref[g * CHUNK : (g + 1) * CHUNK].reshape(CHUNK * list_size, width),
+                (((1,), (1,)), ((), ())),
+                preferred_element_type=jnp.float32,
+            )
+            for i in range(CHUNK):
+                n = g * CHUNK + i
+                hit = place == n + 1.0
+                hit = jnp.concatenate([hit] * (list_size // LANES), axis=1)
+                value = dots[:, i * list_size : (i + 1) * list_size] - norms_ref[n : n + 1, :]
+                best = jnp.where(hit, value, best)
+            for step in relay_after.get((k, g), []):
+                step()
+        encode(p, best, norm)
+        for i in range(1 if k == 0 else 0, PLANE):
+            target = p * PLANE + lax.rem(inside + i, PLANE)
+            copy = back(target, me)
+            copy.start()
+            returned.append(copy)
+    got_ref[me] = send_ref[me]
+
+    target = jnp.where(lane8 < query_count, (stored >> 5).astype(jnp.float32), -1.0)
+    mine = jnp.concatenate(
+        [jnp.where(target == float(d), 1.0, 0.0) for d in range(devices)], axis=0
+    )
+    rank = ranks(mine)
+    spot = jnp.zeros(ids.shape, jnp.float32)
+    for d in range(devices):
+        spot = jnp.where(target == float(d), rank[d * 8 : (d + 1) * 8] + float(d * capacity), spot)
+    wide = lax.broadcasted_iota(jnp.int32, (8, devices * capacity), 1).astype(jnp.float32)
+    for q in range(0, query_count, 2):
+        both = [jnp.where(spot[:, i : i + 1] == wide, 1.0, 0.0) for i in (q, q + 1)]
+        place_ref[q * 8 : (q + 2) * 8, :] = jnp.concatenate(both, axis=0).astype(jnp.bfloat16)
+
+    for p in planes:
+        for i in range(PLANE):
+            block = p * PLANE + lax.rem(inside + i, PLANE)
+            if p is not planes[0] or i > 0:
+                back(block, block).wait_recv()
+
+    words = got_ref[:, :capacity, :].reshape(devices * capacity, LANES)
+    pieces = [(words >> s) & 255 for s in (0, 8, 16, 24)]
+    pieces = [piece.astype(jnp.float32).astype(jnp.bfloat16) for piece in pieces]
+    powers = got_ref[:, capacity : capacity + 1, :].astype(jnp.float32)
+    powers = jnp.sum(powers.reshape(devices // 4, 4, LANES), axis=1)
+    powers = jnp.concatenate(
+        [jnp.broadcast_to(powers[g : g + 1, :], (LANES, LANES)) for g in range(devices // 4)],
+        axis=1,
+    ).astype(jnp.bfloat16)
+    chosen = jnp.dot(
+        place_ref[...], jnp.concatenate(pieces, axis=1), preferred_element_type=jnp.float32
+    )
+    power = lax.dot_general(
+        place_ref[...], powers, (((1,), (1,)), ((), ())), preferred_element_type=jnp.float32
+    )
+    scale = jnp.exp(power * LN2) * (1.0 / 65535.0)
+    for h in range(2):
+        low = chosen[:, 2 * h * LANES : (2 * h + 1) * LANES]
+        high = chosen[:, (2 * h + 1) * LANES : (2 * h + 2) * LANES]
+        out_ref[:, h * LANES : (h + 1) * LANES] = (low + 256.0 * high) * scale
+
+    for copy in sent:
+        copy.wait_send()
+    for copy in returned:
+        copy.wait_send()
+
+
+def fused(queries, projection, lists, probes, owner_map):
+    query_count, width = queries.shape
+    probe_count = probes.shape[1]
+    list_count, list_size = lists.shape[0], lists.shape[1]
+    devices, capacity = PLANES * PLANE, 32
+    rows = width // LANES * query_count + TABLE
+    vmem = pl.BlockSpec(memory_space=pltpu.VMEM)
+    scores = pl.pallas_call(
+        fused_kernel,
+        out_shape=jax.ShapeDtypeStruct((query_count * probe_count, list_size), jnp.float32),
+        in_specs=[vmem, vmem, vmem, vmem, pl.BlockSpec(memory_space=pl.ANY)],
+        out_specs=vmem,
+        scratch_shapes=[
+            pltpu.VMEM((devices, rows, LANES), jnp.bfloat16),
+            pltpu.VMEM(lists.shape, jnp.bfloat16),
+            pltpu.VMEM((list_count, list_size), jnp.float32),
+            pltpu.VMEM((PLANE * capacity, width), jnp.bfloat16),
+            pltpu.VMEM((devices, capacity + 1, LANES), jnp.int32),
+            pltpu.VMEM((devices, capacity + 1, LANES), jnp.int32),
+            pltpu.VMEM((query_count * probe_count, devices * capacity), jnp.bfloat16),
+            pltpu.SemaphoreType.DMA((8,)),
+            pltpu.SemaphoreType.DMA((devices,)),
+            pltpu.SemaphoreType.DMA((devices,)),
+            pltpu.SemaphoreType.DMA((devices,)),
+            pltpu.SemaphoreType.DMA((devices,)),
+        ],
+        compiler_params=pltpu.CompilerParams(
+            collective_id=0, has_side_effects=True, vmem_limit_bytes=52 * 2**20
+        ),
+    )(queries, projection, probes.T, owner_map.reshape(-1, LANES), lists)
+    return scores.reshape(query_count, probe_count, list_size)
+
+
 def solution(mesh):
     placed = (
         P(AXES, None),
@@ -345,6 +620,11 @@
         P(AXES, None),
         P(),
     )
+    sizes = (mesh.shape["grp"], mesh.shape["own"])
     return jax.shard_map(
-        body, mesh=mesh, in_specs=placed, out_specs=P(AXES, None, None), check_vma=False
-    )
+        fused if sizes == (8, 4) else general,
+        mesh=mesh,
+        in_specs=placed,
+        out_specs=P(AXES, None, None),
+        check_vma=False,
+    )

time: 92.4 us -> 52.4 us (0.57)
  the two profiles are of different devices: /device:TPU:11 before, /device:TPU:9 now
where the time goes in v1:
time: 52.4 us; the launch traced here: 52.2 us
  Pallas kernels  47.8 us (91%)
  local copies, waits for them, and re-layouts  4.33 us (8%)
    pallas_call x1, Pallas kernels, fused(): pl.pallas_call(fused_kernel, out_shape=jax.ShapeDtypeStruct((query_count...  47.8 us
    unnamed x9, local copies, waits for them, and re-layouts  4.33 us

profile of v1, /device:TPU:9, one launch (start us, length us, event | category | flops | bytes accessed | tf_op | source)
XLA Modules:
  0.0 52.2 jit_solution(13681395124365464848)
XLA Ops:
  0.0 0.0 copy-start
  0.0 1.3 %copy-done = bf16[768,768]{1,0:T(8,128)(2,1)S(1)} copy-done((bf16[768,768]{1,0:T(8,128)(2,1)S(1)}, bf16[768,768]{1,0:T(8,128)(2,1)}, u32[]{:S(2)}) %copy-start) | copy-done | bytes 1179672
  1.3 0.0 copy-start.1
  1.3 0.9 %copy-done.1 = bf16[64,768]{1,0:T(8,128)(2,1)S(1)} copy-done((bf16[64,768]{1,0:T(8,128)(2,1)S(1)}, bf16[64,768]{1,0:T(8,128)(2,1)}, u32[]{:S(2)}) %copy-start.1) | copy-done | bytes 98328
  2.2 0.0 copy-start.2
  2.2 0.7 %copy-done.2 = s32[64,8]{0,1:T(8,128)S(1)} copy-done((s32[64,8]{0,1:T(8,128)S(1)}, s32[64,8]{0,1:T(8,128)}, u32[]{:S(2)}) %copy-start.2) | copy-done | bytes 2072
  2.9 0.0 copy-start.3
  2.9 0.7 %copy-done.3 = s32[1024]{0:T(1024)S(1)} copy-done((s32[1024]{0:T(1024)S(1)}, s32[1024]{0:T(1024)}, u32[]{:S(2)}) %copy-start.3) | copy-done | bytes 4120
  3.5 47.8 %shard_map.55 = f32[512,256]{1,0:T(8,128)S(1)} custom-call(bf16[64,768]{1,0:T(8,128)(2,1)S(1)} %copy-done.1, bf16[768,768]{1,0:T(8,128)(2,1)S(1)} %copy-done, s32[8,64]{1,0:T(8,128)S(1)} %bitcast.4, s32[8,128]{1,0:T(8,128)S(1)} %bitcast.5, bf16[32,256,768]{2,1,0:T(8,128)(2,1)} %lists_hbm.1), custom_call_target="tpu_custom_call" | custom-call | tf_op jit(solution)/shard_map/pallas_call | solution.py:589
  51.4 0.8 %copy.7 = f32[64,8,256]{2,1,0:T(8,128)} copy(f32[64,8,256]{2,1,0:T(8,128)S(1)} %bitcast.3) | data formatting | bytes 1048576
Async XLA Ops:
  0.0 1.3 %copy-start = (bf16[768,768]{1,0:T(8,128)(2,1)S(1)}, bf16[768,768]{1,0:T(8,128)(2,1)}, u32[]{:S(2)}) copy-start(bf16[768,768]{1,0:T(8,128)(2,1)} %projection_ref.1) | copy-start | bytes 3538948
  1.3 0.9 %copy-start.1 = (bf16[64,768]{1,0:T(8,128)(2,1)S(1)}, bf16[64,768]{1,0:T(8,128)(2,1)}, u32[]{:S(2)}) copy-start(bf16[64,768]{1,0:T(8,128)(2,1)} %queries_ref.1) | copy-start | bytes 294916
  2.2 0.7 %copy-start.2 = (s32[64,8]{0,1:T(8,128)S(1)}, s32[64,8]{0,1:T(8,128)}, u32[]{:S(2)}) copy-start(s32[64,8]{0,1:T(8,128)} %param.8) | copy-start | bytes 6148
  2.9 0.7 %copy-start.3 = (s32[1024]{0:T(1024)S(1)}, s32[1024]{0:T(1024)}, u32[]{:S(2)}) copy-start(s32[1024]{0:T(1024)} %param.9) | copy-start | bytes 12292

commit v2 on v1

--- a/solution.py
+++ b/solution.py
@@ -249,7 +249,9 @@
 PLANES = 4
 PLANE = 8
 TABLE = 16
-CHUNK = 8
+CHIPS = 4
+CAPACITY = 32
+VMEM_LIMIT = 56 * 2**20
 
 
 def number(z, x, y, c):
@@ -261,51 +263,70 @@
 
 
 def ranks(mine):
-    rows = mine.shape[0]
-    lane_a = lax.broadcasted_iota(jnp.int32, (LANES, LANES), 0)
-    lane_b = lax.broadcasted_iota(jnp.int32, (LANES, LANES), 1)
-    upper = jnp.where(lane_a < lane_b, 1.0, 0.0).astype(jnp.bfloat16)
-    ones = jnp.ones((LANES, LANES), jnp.bfloat16)
-    row_a = lax.broadcasted_iota(jnp.int32, (rows, rows), 0)
-    row_b = lax.broadcasted_iota(jnp.int32, (rows, rows), 1)
-    lower = jnp.where((row_a // 8 == row_b // 8) & (row_b < row_a), 1.0, 0.0).astype(jnp.bfloat16)
-    narrow = mine.astype(jnp.bfloat16)
-    within = jnp.dot(narrow, upper, preferred_element_type=jnp.float32)
-    totals = jnp.dot(narrow, ones, preferred_element_type=jnp.float32).astype(jnp.bfloat16)
-    return within + jnp.dot(lower, totals, preferred_element_type=jnp.float32)
+    lane = lax.broadcasted_iota(jnp.int32, mine.shape, 1)
+    within = mine
+    for reach in (1, 2, 4, 8, 16, 32, 64):
+        within = within + jnp.where(lane >= reach, pltpu.roll(within, reach, 1), 0.0)
+    totals = jnp.broadcast_to(within[:, LANES - 1 :], mine.shape).reshape(-1, 8, LANES)
+    probe = lax.broadcasted_iota(jnp.int32, totals.shape, 1)
+    before = totals
+    for reach in (1, 2, 4):
+        before = before + jnp.where(probe >= reach, pltpu.roll(before, reach, 1), 0.0)
+    return within - mine + (before - totals).reshape(mine.shape)
 
 
 def fused_kernel(
+    queries_hbm,
+    projection_hbm,
+    probes_hbm,
+    owner_hbm,
+    lists_hbm,
+    out_hbm,
     queries_ref,
     projection_ref,
     probes_ref,
     owner_ref,
-    lists_hbm,
-    out_ref,
     all_ref,
     lists_ref,
     norms_ref,
-    picked_ref,
+    even_ref,
+    odd_ref,
     send_ref,
     got_ref,
     place_ref,
+    total_ref,
+    out_ref,
+    input_sem,
     list_sem,
     spread_send,
     spread_recv,
     back_send,
     back_recv,
+    out_sem,
 ):
     grp, own = lax.axis_index("grp"), lax.axis_index("own")
     z, x, y, c = grp // 2, lax.rem(grp, 2), own // 2, lax.rem(own, 2)
     me = number(z, x, y, c)
-    inside = x * 4 + y * 2 + c
     devices = all_ref.shape[0]
     query_count, width = queries_ref.shape
     list_count, list_size = lists_ref.shape[0], lists_ref.shape[1]
     columns = width // LANES
     table_at = columns * query_count
-    capacity = 32
-
+    capacity = CAPACITY
+
+    inputs = [
+        pltpu.make_async_copy(src, dst, input_sem.at[i])
+        for i, (src, dst) in enumerate(
+            (
+                (projection_hbm, projection_ref),
+                (queries_hbm, queries_ref),
+                (probes_hbm, probes_ref),
+                (owner_hbm, owner_ref),
+            )
+        )
+    ]
+    for copy in inputs:
+        copy.start()
     barrier = pltpu.get_barrier_semaphore()
 
     @pl.loop(1, devices)
@@ -325,6 +346,8 @@
 
     for n in range(list_sem.shape[0]):
         list_copy(n).start()
+    for copy in inputs:
+        copy.wait()
 
     projected = jnp.dot(
         queries_ref[...], projection_ref[...], preferred_element_type=jnp.float32
@@ -347,13 +370,21 @@
     )
     pl.semaphore_wait(barrier, devices - 1)
 
-    first = 3 * (1 - z // 2)
-    last = 1 + lax.rem(z, 2)
-    planes = [z, first, 6 - z - first - last, last]
+    near, cross, opposite = z + 1 - 2 * lax.rem(z, 2), lax.rem(z + 2, PLANES), PLANES - 1 - z
     xa, ya = x * c + (1 - x) * (1 - c), y * (1 - c) + (1 - y) * c
     xb, yb = x * (1 - c) + (1 - x) * c, y * c + (1 - y) * (1 - c)
-    peer_a, peer_b = number(z, xa, ya, c), number(z, xb, yb, c)
-    sibling = number(z, x, y, 1 - c)
+    sides = {"o": (x, y), "a": (xa, ya), "b": (xb, yb), "d": (1 - x, 1 - y)}
+    sides |= {"x": (1 - x, y), "y": (x, 1 - y)}
+
+    def block_of(p, side):
+        return number(p, *sides[side], c)
+
+    def twin_of(p, side):
+        return number(p, *sides[side], 1 - c)
+
+    peer_a, peer_b = block_of(z, "a"), block_of(z, "b")
+    peer_near, peer_cross = block_of(near, "o"), block_of(cross, "o")
+    sibling = twin_of(z, "o")
     sent = []
 
     def describe(block, peer, slot):
@@ -366,48 +397,22 @@
             device_id_type=pl.DeviceIdType.MESH,
         )
 
-    def send(block, peer):
-        copy = describe(block, peer, len(sent))
-        copy.start()
-        sent.append(copy)
+    def send(block, *peers):
+        for peer in peers:
+            copy = describe(block, peer, len(sent))
+            copy.start()
+            sent.append(copy)
 
     def arrived(block):
         describe(block, sibling, 0).wait_recv()
 
-    def relay_column(p):
-        block = number(p, x, y, c)
-        arrived(block)
-        send(block, peer_a)
-        send(block, peer_b)
-        send(block, sibling)
-
-    def relay_a(p):
-        block = number(p, xa, ya, c)
-        arrived(block)
-        send(block, peer_b)
-        send(block, sibling)
-
-    def relay_b(p):
-        block = number(p, xb, yb, c)
-        arrived(block)
-        send(block, sibling)
-
-    def relay_diagonal(p):
-        block = number(p, 1 - x, 1 - y, c)
-        arrived(block)
-        send(block, sibling)
-
-    def complete(p):
-        for xx, yy in ((x, y), (xa, ya), (xb, yb), (1 - x, 1 - y)):
-            arrived(number(p, xx, yy, 1 - c))
-
-    send(me, peer_a)
-    send(me, peer_b)
-    for p in planes[1:]:
-        send(me, number(p, x, y, c))
-    send(me, sibling)
-
-    def list_norms(n):
+    def relay(p, side, *peers):
+        arrived(block_of(p, side))
+        send(block_of(p, side), *peers)
+
+    send(me, peer_cross, peer_a, peer_b, peer_near, sibling)
+
+    for n in range(list_sem.shape[0]):
         list_copy(n).wait()
         rows = []
         for i in range(n * part, (n + 1) * part):
@@ -418,16 +423,33 @@
             rows.append(0.5 * jnp.sum(partial.T, axis=0, keepdims=True))
         norms_ref[n * part : (n + 1) * part, :] = jnp.concatenate(rows, axis=0)
 
-    steps = {
-        3: lambda: relay_a(planes[0]),
-        4: lambda: relay_b(planes[0]),
-        5: lambda: relay_column(planes[1]),
-        6: lambda: relay_diagonal(planes[0]),
-    }
-    for n in range(list_sem.shape[0]):
-        list_norms(n)
-        if n in steps:
-            steps[n]()
+    relay(z, "a", sibling)
+    relay(z, "b", sibling)
+    relay(cross, "o", peer_near, sibling, peer_a, peer_b)
+    send(peer_a, peer_b)
+
+    batches = (
+        ((z, "o"), (z, "x"), (z, "y"), (cross, "o")),
+        ((cross, "x"), (cross, "y"), (opposite, "o"), (near, "o")),
+        ((cross, "d"), (opposite, "x"), (opposite, "y"), (z, "d")),
+        ((opposite, "d"), (near, "x"), (near, "y"), (near, "d")),
+    )
+    order = [
+        number(p, *sides[side], core).astype(jnp.float32)
+        for chips in batches
+        for p, side in chips
+        for core in range(2)
+    ]
+    target = jnp.where(lane8 < query_count, (stored >> 5).astype(jnp.float32), -1.0)
+    mine = jnp.concatenate([jnp.where(target == d, 1.0, 0.0) for d in order], axis=0)
+    rank = ranks(mine)
+    spot = jnp.zeros(ids.shape, jnp.float32)
+    for n, d in enumerate(order):
+        spot = jnp.where(target == d, rank[n * 8 : (n + 1) * 8] + float(n * capacity), spot)
+    wide = lax.broadcasted_iota(jnp.int32, (8, devices * capacity), 1).astype(jnp.float32)
+    for q in range(0, query_count, 2):
+        both = [jnp.where(spot[:, i : i + 1] == wide, 1.0, 0.0) for i in (q, q + 1)]
+        place_ref[q * 8 : (q + 2) * 8, :] = jnp.concatenate(both, axis=0).astype(jnp.bfloat16)
 
     def back(target, block):
         return pltpu.make_async_remote_copy(
@@ -440,13 +462,18 @@
         )
 
     me_f = me.astype(jnp.float32)
-    slots = PLANE * capacity
-    ones = jnp.ones((LANES, LANES), jnp.bfloat16)
+    slots = 2 * CHIPS * capacity
     slot = lax.broadcasted_iota(jnp.int32, (capacity, LANES), 0).astype(jnp.float32)
 
-    def choose(p):
-        tables = all_ref[pl.ds(p * PLANE, PLANE), table_at:, :].astype(jnp.float32)
-        tables = tables[:, :8, :].reshape(PLANE * 8, LANES)
+    def both_of(place):
+        p, side = place
+        return pl.ds(number(p, *sides[side], 0), 2)
+
+    def choose(chips):
+        tables = [
+            all_ref[both_of(chip), table_at:, :].astype(jnp.float32)[:, :8, :] for chip in chips
+        ]
+        tables = jnp.concatenate(tables, axis=0).reshape(2 * CHIPS * 8, LANES)
         lane = lax.broadcasted_iota(jnp.int32, tables.shape, 1)
         mine = jnp.where((lane < query_count) & (tables == me_f), 1.0, 0.0)
         rank = jnp.where(mine > 0.5, ranks(mine), -1.0)
@@ -454,7 +481,7 @@
         at = (rank, pltpu.roll(rank, query_count, 1))
         what = (pltpu.roll(local, query_count, 1), local)
         picks, lists_of = [], []
-        for t in range(PLANE):
+        for t in range(2 * CHIPS):
             pick = jnp.zeros((capacity, LANES), jnp.float32)
             which = jnp.zeros((capacity, LANES), jnp.float32)
             for j in range(8):
@@ -463,152 +490,217 @@
                 pick = jnp.where(hit, 1.0, pick)
                 which = jnp.where(hit, what[t % 2][row : row + 1, :], which)
             picks.append(pick.astype(jnp.bfloat16))
-            lists_of.append(which.astype(jnp.bfloat16))
-        place = jnp.dot(
-            jnp.concatenate(lists_of, axis=0), ones, preferred_element_type=jnp.float32
-        )
+            lists_of.append(which)
+        place = jnp.sum(jnp.concatenate(lists_of, axis=0), axis=1, keepdims=True)
+        place = jnp.broadcast_to(place, (slots, LANES))
+        return picks, place
+
+    def select(chips, picks, picked):
         norm = jnp.zeros((slots, LANES), jnp.float32)
         for j in range(columns):
             rows = []
-            for u in range(PLANE // 2):
+            for u, chip in enumerate(chips):
                 pair = all_ref[
-                    pl.ds(p * PLANE + 2 * u, 2), j * query_count : (j + 1) * query_count, :
+                    both_of(chip), j * query_count : (j + 1) * query_count, :
                 ].reshape(2 * query_count, LANES)
                 pick = jnp.concatenate(picks[2 * u : 2 * u + 2], axis=0)
                 rows.append(jnp.dot(pick, pair, preferred_element_type=jnp.float32))
             piece = jnp.concatenate(rows, axis=0)
             norm = norm + piece * piece
-            picked_ref[:, j * LANES : (j + 1) * LANES] = piece.astype(jnp.bfloat16)
-        return place, jnp.sum(norm, axis=1, keepdims=True)
-
-    def encode(p, best, norm):
+            picked[:, j * LANES : (j + 1) * LANES] = piece.astype(jnp.bfloat16)
+        return jnp.sum(norm, axis=1, keepdims=True)
+
+    def encode(chips, best, norm):
         distance = jnp.maximum((norm - 2.0 * best) * (1.0 / width), 0.0)
         largest = jnp.maximum(jnp.max(distance, axis=1, keepdims=True), 1e-30)
         power = jnp.clip(jnp.ceil(jnp.log(largest) * LOG2E + 1e-3), -100.0, 120.0)
         code = jnp.clip(jnp.round(distance * (65535.0 * jnp.exp(power * -LN2))), 0.0, 65535.0)
         code = code.astype(jnp.int32)
         word = code[:, :LANES] | (code[:, LANES:] << 16)
-        here = pl.ds(p * PLANE, PLANE)
-        send_ref[here, :capacity, :] = word.reshape(PLANE, capacity, LANES)
-        spot = lax.broadcasted_iota(jnp.int32, (PLANE, capacity, LANES), 1) + own * capacity
-        lane = lax.broadcasted_iota(jnp.int32, (PLANE, capacity, LANES), 2)
-        powers = jnp.broadcast_to(power, (slots, LANES)).reshape(PLANE, capacity, LANES)
+        word = word.reshape(2 * CHIPS, capacity, LANES)
+        whole = (2 * CHIPS, capacity, LANES)
+        half = lax.broadcasted_iota(jnp.int32, whole, 0) // 2
+        half = (half - 2 * (half // 2)) * 2 + c
+        spot = lax.broadcasted_iota(jnp.int32, whole, 1) + half * capacity
+        lane = lax.broadcasted_iota(jnp.int32, whole, 2)
+        powers = jnp.broadcast_to(power, (slots, LANES)).reshape(whole)
         powers = jnp.sum(jnp.where(spot == lane, powers, 0.0), axis=1, keepdims=True)
-        send_ref[here, capacity : capacity + 1, :] = powers.astype(jnp.int32)
-
-    relay_after = {}
-    for k in range(PLANES - 1):
-        later = planes[k + 1]
-        relay_after[k, 0] = [lambda p=later: relay_a(p)]
-        relay_after[k, 1] = [lambda p=later: relay_b(p)]
-        if k + 2 < PLANES:
-            relay_after[k, 1].append(lambda p=planes[k + 2]: relay_column(p))
-        relay_after[k, 2] = [lambda p=later: relay_diagonal(p)]
+        powers = powers.astype(jnp.int32)
+        for u, chip in enumerate(chips):
+            send_ref[both_of(chip), :capacity, :] = word[2 * u : 2 * u + 2]
+            send_ref[both_of(chip), capacity : capacity + 1, :] = powers[2 * u : 2 * u + 2]
 
     returned = []
-    for k, p in enumerate(planes):
-        complete(p)
-        place, norm = choose(p)
+
+    def ends(p, side):
+        own_chip = p is z and side == "o"
+        return [twin_of(p, side)] if own_chip else [block_of(p, side), twin_of(p, side)]
+
+    def give_back(chips):
+        for p, side in chips:
+            for block in ends(p, side):
+                copy = back(block, me)
+                copy.start()
+                returned.append(copy)
+
+    half = (
+        (
+            (cross, "a", peer_b, sibling),
+            (cross, "b", sibling),
+            (opposite, "o", sibling, peer_a, peer_b),
+            (near, "o", sibling, peer_a, peer_b),
+            (z, "d", sibling),
+        ),
+        (
+            (cross, "d", sibling),
+            (opposite, "a", sibling, peer_b),
+            (opposite, "b", sibling),
+        ),
+        (),
+        (),
+    )
+    late = ((), ((near, "a", peer_b, sibling), (near, "b", sibling)), (), ())
+    soon = ((), (), ((opposite, "d", sibling), (near, "d", sibling)), ())
+    picked_refs = (even_ref, odd_ref)
+
+    def prepare(k):
+        for p, side in batches[k]:
+            arrived(twin_of(p, side))
+        return choose(batches[k])
+
+    def score(k, place, best, first, count):
+        dots = lax.dot_general(
+            picked_refs[k % 2][...],
+            lists_ref[first : first + count].reshape(count * list_size, width),
+            (((1,), (1,)), ((), ())),
+            preferred_element_type=jnp.float32,
+        )
+        for i in range(count):
+            n = first + i
+            hit = place == n + 1.0
+            hit = jnp.concatenate([hit] * (list_size // LANES), axis=1)
+            value = dots[:, i * list_size : (i + 1) * list_size] - norms_ref[n : n + 1, :]
+            best = jnp.where(hit, value, best)
+        return best
+
+    step = list_count // 4
+    picks, place = prepare(0)
+    norm = select(batches[0], picks, picked_refs[0])
+    for k, chips in enumerate(batches):
         best = jnp.zeros((slots, list_size), jnp.float32)
-        for g in range(list_count // CHUNK):
-            dots = lax.dot_general(
-                picked_ref[...],
-                lists_ref[g * CHUNK : (g + 1) * CHUNK].reshape(CHUNK * list_size, width),
-                (((1,), (1,)), ((), ())),
-                preferred_element_type=jnp.float32,
-            )
-            for i in range(CHUNK):
-                n = g * CHUNK + i
-                hit = place == n + 1.0
-                hit = jnp.concatenate([hit] * (list_size // LANES), axis=1)
-                value = dots[:, i * list_size : (i + 1) * list_size] - norms_ref[n : n + 1, :]
-                best = jnp.where(hit, value, best)
-            for step in relay_after.get((k, g), []):
-                step()
-        encode(p, best, norm)
-        for i in range(1 if k == 0 else 0, PLANE):
-            target = p * PLANE + lax.rem(inside + i, PLANE)
-            copy = back(target, me)
-            copy.start()
-            returned.append(copy)
+        begin = 0
+        for stop, relayed in ((1, soon[k]), (2, half[k]), (3, late[k])):
+            if relayed or (stop == 3 and 0 < k < 3):
+                best = score(k, place, best, begin * step, (stop - begin) * step)
+                begin = stop
+                for item in relayed:
+                    relay(*item)
+        ahead = 0 < k < len(batches) - 1
+        if ahead:
+            picks, later = prepare(k + 1)
+        best = score(k, place, best, begin * step, (4 - begin) * step)
+        if ahead:
+            after = select(batches[k + 1], picks, picked_refs[(k + 1) % 2])
+        encode(chips, best, norm)
+        give_back(chips)
+        if k == 0:
+            picks, later = prepare(1)
+            after = select(batches[1], picks, picked_refs[1])
+        place, norm = later, after
     got_ref[me] = send_ref[me]
 
-    target = jnp.where(lane8 < query_count, (stored >> 5).astype(jnp.float32), -1.0)
-    mine = jnp.concatenate(
-        [jnp.where(target == float(d), 1.0, 0.0) for d in range(devices)], axis=0
-    )
-    rank = ranks(mine)
-    spot = jnp.zeros(ids.shape, jnp.float32)
-    for d in range(devices):
-        spot = jnp.where(target == float(d), rank[d * 8 : (d + 1) * 8] + float(d * capacity), spot)
-    wide = lax.broadcasted_iota(jnp.int32, (8, devices * capacity), 1).astype(jnp.float32)
-    for q in range(0, query_count, 2):
-        both = [jnp.where(spot[:, i : i + 1] == wide, 1.0, 0.0) for i in (q, q + 1)]
-        place_ref[q * 8 : (q + 2) * 8, :] = jnp.concatenate(both, axis=0).astype(jnp.bfloat16)
-
-    for p in planes:
-        for i in range(PLANE):
-            block = p * PLANE + lax.rem(inside + i, PLANE)
-            if p is not planes[0] or i > 0:
+    def receive(chips):
+        for p, side in chips:
+            for block in ends(p, side):
                 back(block, block).wait_recv()
 
-    words = got_ref[:, :capacity, :].reshape(devices * capacity, LANES)
-    pieces = [(words >> s) & 255 for s in (0, 8, 16, 24)]
-    pieces = [piece.astype(jnp.float32).astype(jnp.bfloat16) for piece in pieces]
-    powers = got_ref[:, capacity : capacity + 1, :].astype(jnp.float32)
-    powers = jnp.sum(powers.reshape(devices // 4, 4, LANES), axis=1)
-    powers = jnp.concatenate(
-        [jnp.broadcast_to(powers[g : g + 1, :], (LANES, LANES)) for g in range(devices // 4)],
-        axis=1,
-    ).astype(jnp.bfloat16)
-    chosen = jnp.dot(
-        place_ref[...], jnp.concatenate(pieces, axis=1), preferred_element_type=jnp.float32
-    )
-    power = lax.dot_general(
-        place_ref[...], powers, (((1,), (1,)), ((), ())), preferred_element_type=jnp.float32
-    )
-    scale = jnp.exp(power * LN2) * (1.0 / 65535.0)
+    def unpack(some, k):
+        codes, powers = [], []
+        for chips in some:
+            words = jnp.concatenate([got_ref[both_of(chip), :capacity, :] for chip in chips], axis=0)
+            words = words.reshape(slots, LANES)
+            pieces = [((words >> s) & 255).astype(jnp.float32) for s in (0, 8, 16, 24)]
+            codes.append(jnp.concatenate([p.astype(jnp.bfloat16) for p in pieces], axis=1))
+            for u in range(0, CHIPS, 2):
+                rows = [
+                    got_ref[both_of(chip), capacity : capacity + 1, :].astype(jnp.float32)
+                    for chip in chips[u : u + 2]
+                ]
+                row = jnp.sum(jnp.concatenate(rows, axis=0), axis=0)
+                powers.append(jnp.broadcast_to(row, (LANES, LANES)).astype(jnp.bfloat16))
+        place = place_ref[:, k * slots : (k + len(some)) * slots]
+        chosen = jnp.dot(
+            place, jnp.concatenate(codes, axis=0), preferred_element_type=jnp.float32
+        )
+        power = lax.dot_general(
+            place,
+            jnp.concatenate(powers, axis=1),
+            (((1,), (1,)), ((), ())),
+            preferred_element_type=jnp.float32,
+        )
+        return jnp.concatenate([chosen, power], axis=1)
+
+    for chips in batches[:-1]:
+        receive(chips)
+    total_ref[...] = unpack(batches[:-1], 0)
+    receive(batches[-1])
+    total = total_ref[...] + unpack(batches[-1:], len(batches) - 1)
+    scale = jnp.exp(total[:, 4 * LANES :] * LN2) * (1.0 / 65535.0)
     for h in range(2):
-        low = chosen[:, 2 * h * LANES : (2 * h + 1) * LANES]
-        high = chosen[:, (2 * h + 1) * LANES : (2 * h + 2) * LANES]
+        low = total[:, 2 * h * LANES : (2 * h + 1) * LANES]
+        high = total[:, (2 * h + 1) * LANES : (2 * h + 2) * LANES]
         out_ref[:, h * LANES : (h + 1) * LANES] = (low + 256.0 * high) * scale
-
+    result = pltpu.make_async_copy(out_ref, out_hbm, out_sem)
+    result.start()
     for copy in sent:
         copy.wait_send()
     for copy in returned:
         copy.wait_send()
+    result.wait()
 
 
 def fused(queries, projection, lists, probes, owner_map):
     query_count, width = queries.shape
     probe_count = probes.shape[1]
     list_count, list_size = lists.shape[0], lists.shape[1]
-    devices, capacity = PLANES * PLANE, 32
+    devices = PLANES * PLANE
+    pairs, slots = query_count * probe_count, devices * CAPACITY
     rows = width // LANES * query_count + TABLE
-    vmem = pl.BlockSpec(memory_space=pltpu.VMEM)
+    hbm = pl.BlockSpec(memory_space=pltpu.HBM)
+    owners = owner_map.reshape(-1, LANES)
+    words = (devices, CAPACITY + 1, LANES)
     scores = pl.pallas_call(
         fused_kernel,
-        out_shape=jax.ShapeDtypeStruct((query_count * probe_count, list_size), jnp.float32),
-        in_specs=[vmem, vmem, vmem, vmem, pl.BlockSpec(memory_space=pl.ANY)],
-        out_specs=vmem,
+        out_shape=jax.ShapeDtypeStruct((pairs, list_size), jnp.float32),
+        in_specs=[hbm] * 5,
+        out_specs=hbm,
         scratch_shapes=[
+            pltpu.VMEM(queries.shape, jnp.bfloat16),
+            pltpu.VMEM(projection.shape, jnp.bfloat16),
+            pltpu.VMEM((probe_count, query_count), jnp.int32),
+            pltpu.VMEM(owners.shape, jnp.int32),
             pltpu.VMEM((devices, rows, LANES), jnp.bfloat16),
             pltpu.VMEM(lists.shape, jnp.bfloat16),
             pltpu.VMEM((list_count, list_size), jnp.float32),
-            pltpu.VMEM((PLANE * capacity, width), jnp.bfloat16),
-            pltpu.VMEM((devices, capacity + 1, LANES), jnp.int32),
-            pltpu.VMEM((devices, capacity + 1, LANES), jnp.int32),
-            pltpu.VMEM((query_count * probe_count, devices * capacity), jnp.bfloat16),
+            pltpu.VMEM((2 * CHIPS * CAPACITY, width), jnp.bfloat16),
+            pltpu.VMEM((2 * CHIPS * CAPACITY, width), jnp.bfloat16),
+            pltpu.VMEM(words, jnp.int32),
+            pltpu.VMEM(words, jnp.int32),
+            pltpu.VMEM((pairs, slots), jnp.bfloat16),
+            pltpu.VMEM((pairs, 5 * LANES), jnp.float32),
+            pltpu.VMEM((pairs, list_size), jnp.float32),
+            pltpu.SemaphoreType.DMA((4,)),
             pltpu.SemaphoreType.DMA((8,)),
             pltpu.SemaphoreType.DMA((devices,)),
             pltpu.SemaphoreType.DMA((devices,)),
             pltpu.SemaphoreType.DMA((devices,)),
             pltpu.SemaphoreType.DMA((devices,)),
+            pltpu.SemaphoreType.DMA,
         ],
         compiler_params=pltpu.CompilerParams(
-            collective_id=0, has_side_effects=True, vmem_limit_bytes=52 * 2**20
+            collective_id=0, has_side_effects=True, vmem_limit_bytes=VMEM_LIMIT
         ),
-    )(queries, projection, probes.T, owner_map.reshape(-1, LANES), lists)
+    )(queries, projection, probes.T, owners, lists)
     return scores.reshape(query_count, probe_count, list_size)
 
 

time: 52.4 us -> 46 us (0.88)
  the two profiles are of different devices: /device:TPU:9 before, /device:TPU:0 now
where the time goes in v2:
time: 46 us; the launch traced here: 45.8 us
  Pallas kernels  43.9 us (95%)
  local copies, waits for them, and re-layouts  1.87 us (4%)
    pallas_call x1, Pallas kernels, fused(): pl.pallas_call(fused_kernel, out_shape=jax.ShapeDtypeStruct((pairs, list_...  43.9 us
    unnamed x1, local copies, waits for them, and re-layouts  1.87 us

profile of v2, /device:TPU:0, one launch (start us, length us, event | category | flops | bytes accessed | tf_op | source)
XLA Modules:
  0.0 45.8 jit_solution(6384951389296041528)
XLA Ops:
  0.0 43.9 %shard_map.55 = f32[512,256]{1,0:T(8,128)} custom-call(bf16[64,768]{1,0:T(8,128)(2,1)} %queries_hbm.1, bf16[768,768]{1,0:T(8,128)(2,1)} %projection_hbm.1, s32[8,64]{1,0:T(8,128)} %bitcast.4, s32[8,128]{1,0:T(8,128)} %bitcast.5, bf16[32,256,768]{2,1,0:T(8,128)(2,1)} %lists_hbm.1), custom_call_target="tpu_custom_call" | custom-call | tf_op jit(solution)/shard_map/pallas_call | solution.py:672
  43.9 1.9 %copy.7 = f32[64,8,256]{2,1,0:T(8,128)} copy(f32[64,8,256]{2,1,0:T(8,128)} %bitcast.3) | data formatting | bytes 1048576

commit v3 on v2

--- a/solution.py
+++ b/solution.py
@@ -249,7 +249,7 @@
 PLANES = 4
 PLANE = 8
 TABLE = 16
-CHIPS = 4
+BATCH = 8
 CAPACITY = 32
 VMEM_LIMIT = 56 * 2**20
 
@@ -329,13 +329,22 @@
         copy.start()
     barrier = pltpu.get_barrier_semaphore()
 
-    @pl.loop(1, devices)
-    def _(k):
+    near, cross, opposite = z + 1 - 2 * lax.rem(z, 2), lax.rem(z + 2, PLANES), PLANES - 1 - z
+    xa, ya = x * c + (1 - x) * (1 - c), y * (1 - c) + (1 - y) * c
+    xb, yb = x * (1 - c) + (1 - x) * c, y * c + (1 - y) * (1 - c)
+    sides = {"o": (x, y), "a": (xa, ya), "b": (xb, yb), "d": (1 - x, 1 - y)}
+    sides |= {"x": (1 - x, y), "y": (x, 1 - y)}
+
+    def block_of(p, side, twin=False):
+        return number(p, *sides[side], 1 - c if twin else c)
+
+    peer_a, peer_b = block_of(z, "a"), block_of(z, "b")
+    peer_near, peer_cross = block_of(near, "o"), block_of(cross, "o")
+    sibling = block_of(z, "o", True)
+    peers = (peer_cross, peer_a, peer_b, peer_near, sibling)
+    for peer in peers:
         pl.semaphore_signal(
-            barrier,
-            inc=1,
-            device_id=mesh_id(lax.rem(me + k, devices)),
-            device_id_type=pl.DeviceIdType.MESH,
+            barrier, inc=1, device_id=mesh_id(peer), device_id_type=pl.DeviceIdType.MESH
         )
 
     part = list_count // list_sem.shape[0]
@@ -368,23 +377,8 @@
     all_ref[me, table_at:, :] = jnp.concatenate([table, jnp.zeros_like(table)], axis=0).astype(
         jnp.bfloat16
     )
-    pl.semaphore_wait(barrier, devices - 1)
-
-    near, cross, opposite = z + 1 - 2 * lax.rem(z, 2), lax.rem(z + 2, PLANES), PLANES - 1 - z
-    xa, ya = x * c + (1 - x) * (1 - c), y * (1 - c) + (1 - y) * c
-    xb, yb = x * (1 - c) + (1 - x) * c, y * c + (1 - y) * (1 - c)
-    sides = {"o": (x, y), "a": (xa, ya), "b": (xb, yb), "d": (1 - x, 1 - y)}
-    sides |= {"x": (1 - x, y), "y": (x, 1 - y)}
-
-    def block_of(p, side):
-        return number(p, *sides[side], c)
-
-    def twin_of(p, side):
-        return number(p, *sides[side], 1 - c)
-
-    peer_a, peer_b = block_of(z, "a"), block_of(z, "b")
-    peer_near, peer_cross = block_of(near, "o"), block_of(cross, "o")
-    sibling = twin_of(z, "o")
+    pl.semaphore_wait(barrier, len(peers))
+
     sent = []
 
     def describe(block, peer, slot):
@@ -410,7 +404,7 @@
         arrived(block_of(p, side))
         send(block_of(p, side), *peers)
 
-    send(me, peer_cross, peer_a, peer_b, peer_near, sibling)
+    send(me, *peers)
 
     for n in range(list_sem.shape[0]):
         list_copy(n).wait()
@@ -425,21 +419,53 @@
 
     relay(z, "a", sibling)
     relay(z, "b", sibling)
-    relay(cross, "o", peer_near, sibling, peer_a, peer_b)
+    relay(cross, "o", peer_a, peer_b, sibling, peer_near)
     send(peer_a, peer_b)
 
+    itself = (z, "o")
     batches = (
-        ((z, "o"), (z, "x"), (z, "y"), (cross, "o")),
-        ((cross, "x"), (cross, "y"), (opposite, "o"), (near, "o")),
-        ((cross, "d"), (opposite, "x"), (opposite, "y"), (z, "d")),
-        ((opposite, "d"), (near, "x"), (near, "y"), (near, "d")),
-    )
-    order = [
-        number(p, *sides[side], core).astype(jnp.float32)
-        for chips in batches
-        for p, side in chips
-        for core in range(2)
-    ]
+        (
+            itself,
+            (z, "o", True),
+            (z, "x"),
+            (z, "x", True),
+            (z, "y"),
+            (z, "y", True),
+            (cross, "o"),
+            (cross, "o", True),
+        ),
+        (
+            (cross, "x"),
+            (cross, "x", True),
+            (cross, "y"),
+            (cross, "y", True),
+            (opposite, "o"),
+            (opposite, "o", True),
+            (near, "o"),
+            (near, "o", True),
+        ),
+        (
+            (cross, "d"),
+            (cross, "d", True),
+            (opposite, "x"),
+            (opposite, "x", True),
+            (opposite, "y"),
+            (opposite, "y", True),
+            (z, "d"),
+            (near, "x"),
+        ),
+        (
+            (opposite, "d"),
+            (opposite, "d", True),
+            (z, "d", True),
+            (near, "x", True),
+            (near, "y"),
+            (near, "y", True),
+            (near, "d"),
+            (near, "d", True),
+        ),
+    )
+    order = [block_of(*where).astype(jnp.float32) for chips in batches for where in chips]
     target = jnp.where(lane8 < query_count, (stored >> 5).astype(jnp.float32), -1.0)
     mine = jnp.concatenate([jnp.where(target == d, 1.0, 0.0) for d in order], axis=0)
     rank = ranks(mine)
@@ -451,29 +477,25 @@
         both = [jnp.where(spot[:, i : i + 1] == wide, 1.0, 0.0) for i in (q, q + 1)]
         place_ref[q * 8 : (q + 2) * 8, :] = jnp.concatenate(both, axis=0).astype(jnp.bfloat16)
 
-    def back(target, block):
+    def back(n):
         return pltpu.make_async_remote_copy(
-            src_ref=send_ref.at[target],
-            dst_ref=got_ref.at[block],
-            send_sem=back_send.at[target],
-            recv_sem=back_recv.at[block],
-            device_id=mesh_id(target),
+            src_ref=send_ref.at[n],
+            dst_ref=got_ref.at[n],
+            send_sem=back_send.at[n],
+            recv_sem=back_recv.at[n],
+            device_id=mesh_id(block_of(*batches[n // BATCH][n % BATCH])),
             device_id_type=pl.DeviceIdType.MESH,
         )
 
     me_f = me.astype(jnp.float32)
-    slots = 2 * CHIPS * capacity
+    slots = BATCH * capacity
     slot = lax.broadcasted_iota(jnp.int32, (capacity, LANES), 0).astype(jnp.float32)
-
-    def both_of(place):
-        p, side = place
-        return pl.ds(number(p, *sides[side], 0), 2)
 
     def choose(chips):
         tables = [
-            all_ref[both_of(chip), table_at:, :].astype(jnp.float32)[:, :8, :] for chip in chips
+            all_ref[block_of(*where), table_at:, :].astype(jnp.float32)[:8, :] for where in chips
         ]
-        tables = jnp.concatenate(tables, axis=0).reshape(2 * CHIPS * 8, LANES)
+        tables = jnp.concatenate(tables, axis=0)
         lane = lax.broadcasted_iota(jnp.int32, tables.shape, 1)
         mine = jnp.where((lane < query_count) & (tables == me_f), 1.0, 0.0)
         rank = jnp.where(mine > 0.5, ranks(mine), -1.0)
@@ -481,7 +503,7 @@
         at = (rank, pltpu.roll(rank, query_count, 1))
         what = (pltpu.roll(local, query_count, 1), local)
         picks, lists_of = [], []
-        for t in range(2 * CHIPS):
+        for t in range(BATCH):
             pick = jnp.zeros((capacity, LANES), jnp.float32)
             which = jnp.zeros((capacity, LANES), jnp.float32)
             for j in range(8):
@@ -499,73 +521,69 @@
         norm = jnp.zeros((slots, LANES), jnp.float32)
         for j in range(columns):
             rows = []
-            for u, chip in enumerate(chips):
-                pair = all_ref[
-                    both_of(chip), j * query_count : (j + 1) * query_count, :
-                ].reshape(2 * query_count, LANES)
-                pick = jnp.concatenate(picks[2 * u : 2 * u + 2], axis=0)
+            for u in range(0, BATCH, 2):
+                pair = [
+                    all_ref[block_of(*where), j * query_count : (j + 1) * query_count, :]
+                    for where in chips[u : u + 2]
+                ]
+                pair = jnp.concatenate(pair, axis=0)
+                pick = jnp.concatenate(picks[u : u + 2], axis=0)
                 rows.append(jnp.dot(pick, pair, preferred_element_type=jnp.float32))
             piece = jnp.concatenate(rows, axis=0)
             norm = norm + piece * piece
             picked[:, j * LANES : (j + 1) * LANES] = piece.astype(jnp.bfloat16)
         return jnp.sum(norm, axis=1, keepdims=True)
 
-    def encode(chips, best, norm):
+    def encode(k, best, norm):
         distance = jnp.maximum((norm - 2.0 * best) * (1.0 / width), 0.0)
         largest = jnp.maximum(jnp.max(distance, axis=1, keepdims=True), 1e-30)
         power = jnp.clip(jnp.ceil(jnp.log(largest) * LOG2E + 1e-3), -100.0, 120.0)
         code = jnp.clip(jnp.round(distance * (65535.0 * jnp.exp(power * -LN2))), 0.0, 65535.0)
         code = code.astype(jnp.int32)
         word = code[:, :LANES] | (code[:, LANES:] << 16)
-        word = word.reshape(2 * CHIPS, capacity, LANES)
-        whole = (2 * CHIPS, capacity, LANES)
-        half = lax.broadcasted_iota(jnp.int32, whole, 0) // 2
-        half = (half - 2 * (half // 2)) * 2 + c
-        spot = lax.broadcasted_iota(jnp.int32, whole, 1) + half * capacity
+        whole = (BATCH, capacity, LANES)
+        word = word.reshape(whole)
+        quarter = lax.broadcasted_iota(jnp.int32, whole, 0) & 3
+        spot = lax.broadcasted_iota(jnp.int32, whole, 1) + quarter * capacity
         lane = lax.broadcasted_iota(jnp.int32, whole, 2)
         powers = jnp.broadcast_to(power, (slots, LANES)).reshape(whole)
         powers = jnp.sum(jnp.where(spot == lane, powers, 0.0), axis=1, keepdims=True)
         powers = powers.astype(jnp.int32)
-        for u, chip in enumerate(chips):
-            send_ref[both_of(chip), :capacity, :] = word[2 * u : 2 * u + 2]
-            send_ref[both_of(chip), capacity : capacity + 1, :] = powers[2 * u : 2 * u + 2]
+        send_ref[k * BATCH : (k + 1) * BATCH, :capacity, :] = word
+        send_ref[k * BATCH : (k + 1) * BATCH, capacity : capacity + 1, :] = powers
 
     returned = []
 
-    def ends(p, side):
-        own_chip = p is z and side == "o"
-        return [twin_of(p, side)] if own_chip else [block_of(p, side), twin_of(p, side)]
-
-    def give_back(chips):
-        for p, side in chips:
-            for block in ends(p, side):
-                copy = back(block, me)
-                copy.start()
-                returned.append(copy)
-
-    half = (
-        (
+    def others(k):
+        return [back(n) for n in range(max(k * BATCH, 1), (k + 1) * BATCH)]
+
+    def give_back(k):
+        for copy in others(k):
+            copy.start()
+            returned.append(copy)
+
+    relays = {
+        (0, 3): (
             (cross, "a", peer_b, sibling),
             (cross, "b", sibling),
-            (opposite, "o", sibling, peer_a, peer_b),
-            (near, "o", sibling, peer_a, peer_b),
-            (z, "d", sibling),
+            (opposite, "o", peer_a, peer_b, sibling),
+            (z, "d", peer_near, sibling),
         ),
-        (
-            (cross, "d", sibling),
-            (opposite, "a", sibling, peer_b),
+        (1, 2): (
+            (cross, "d", peer_near, sibling),
+            (opposite, "a", sibling),
             (opposite, "b", sibling),
+            (near, "a", sibling),
+            (near, "b", sibling),
         ),
-        (),
-        (),
-    )
-    late = ((), ((near, "a", peer_b, sibling), (near, "b", sibling)), (), ())
-    soon = ((), (), ((opposite, "d", sibling), (near, "d", sibling)), ())
+        (2, 1): ((near, "d", sibling), (opposite, "d", sibling)),
+    }
     picked_refs = (even_ref, odd_ref)
 
     def prepare(k):
-        for p, side in batches[k]:
-            arrived(twin_of(p, side))
+        for where in batches[k]:
+            if len(where) == 3:
+                arrived(block_of(*where))
         return choose(batches[k])
 
     def score(k, place, best, first, count):
@@ -584,12 +602,17 @@
         return best
 
     step = list_count // 4
-    picks, place = prepare(0)
+    for where in batches[0]:
+        if len(where) == 3:
+            arrived(block_of(*where))
+    relay(near, "o", peer_a, peer_b, sibling)
+    picks, place = choose(batches[0])
     norm = select(batches[0], picks, picked_refs[0])
     for k, chips in enumerate(batches):
         best = jnp.zeros((slots, list_size), jnp.float32)
         begin = 0
-        for stop, relayed in ((1, soon[k]), (2, half[k]), (3, late[k])):
+        for stop in (1, 2, 3):
+            relayed = relays.get((k, stop), ())
             if relayed or (stop == 3 and 0 < k < 3):
                 best = score(k, place, best, begin * step, (stop - begin) * step)
                 begin = stop
@@ -601,50 +624,44 @@
         best = score(k, place, best, begin * step, (4 - begin) * step)
         if ahead:
             after = select(batches[k + 1], picks, picked_refs[(k + 1) % 2])
-        encode(chips, best, norm)
-        give_back(chips)
+        encode(k, best, norm)
+        give_back(k)
         if k == 0:
             picks, later = prepare(1)
             after = select(batches[1], picks, picked_refs[1])
         place, norm = later, after
-    got_ref[me] = send_ref[me]
-
-    def receive(chips):
-        for p, side in chips:
-            for block in ends(p, side):
-                back(block, block).wait_recv()
-
-    def unpack(some, k):
-        codes, powers = [], []
-        for chips in some:
-            words = jnp.concatenate([got_ref[both_of(chip), :capacity, :] for chip in chips], axis=0)
-            words = words.reshape(slots, LANES)
-            pieces = [((words >> s) & 255).astype(jnp.float32) for s in (0, 8, 16, 24)]
-            codes.append(jnp.concatenate([p.astype(jnp.bfloat16) for p in pieces], axis=1))
-            for u in range(0, CHIPS, 2):
-                rows = [
-                    got_ref[both_of(chip), capacity : capacity + 1, :].astype(jnp.float32)
-                    for chip in chips[u : u + 2]
-                ]
-                row = jnp.sum(jnp.concatenate(rows, axis=0), axis=0)
-                powers.append(jnp.broadcast_to(row, (LANES, LANES)).astype(jnp.bfloat16))
-        place = place_ref[:, k * slots : (k + len(some)) * slots]
-        chosen = jnp.dot(
-            place, jnp.concatenate(codes, axis=0), preferred_element_type=jnp.float32
-        )
+    got_ref[0] = send_ref[0]
+
+    def receive(k):
+        for copy in others(k):
+            copy.wait_recv()
+
+    def unpack(k, count):
+        mine = slice(k * BATCH, (k + count) * BATCH)
+        words = got_ref[mine, :capacity, :].reshape(count * slots, LANES)
+        codes = [((words >> s) & 255).astype(jnp.float32) for s in (0, 8, 16, 24)]
+        codes = jnp.concatenate([p.astype(jnp.bfloat16) for p in codes], axis=1)
+        powers = got_ref[mine, capacity : capacity + 1, :].astype(jnp.float32)
+        powers = jnp.sum(powers.reshape(count * BATCH // 4, 4, LANES), axis=1)
+        powers = jnp.concatenate(
+            [jnp.broadcast_to(powers[g : g + 1], (LANES, LANES)) for g in range(powers.shape[0])],
+            axis=1,
+        ).astype(jnp.bfloat16)
+        place = place_ref[:, k * slots : (k + count) * slots]
+        chosen = jnp.dot(place, codes, preferred_element_type=jnp.float32)
         power = lax.dot_general(
             place,
-            jnp.concatenate(powers, axis=1),
+            powers,
             (((1,), (1,)), ((), ())),
             preferred_element_type=jnp.float32,
         )
         return jnp.concatenate([chosen, power], axis=1)
 
-    for chips in batches[:-1]:
-        receive(chips)
-    total_ref[...] = unpack(batches[:-1], 0)
-    receive(batches[-1])
-    total = total_ref[...] + unpack(batches[-1:], len(batches) - 1)
+    for k in range(len(batches) - 1):
+        receive(k)
+    total_ref[...] = unpack(0, len(batches) - 1)
+    receive(len(batches) - 1)
+    total = total_ref[...] + unpack(len(batches) - 1, 1)
     scale = jnp.exp(total[:, 4 * LANES :] * LN2) * (1.0 / 65535.0)
     for h in range(2):
         low = total[:, 2 * h * LANES : (2 * h + 1) * LANES]
@@ -682,8 +699,8 @@
             pltpu.VMEM((devices, rows, LANES), jnp.bfloat16),
             pltpu.VMEM(lists.shape, jnp.bfloat16),
             pltpu.VMEM((list_count, list_size), jnp.float32),
-            pltpu.VMEM((2 * CHIPS * CAPACITY, width), jnp.bfloat16),
-            pltpu.VMEM((2 * CHIPS * CAPACITY, width), jnp.bfloat16),
+            pltpu.VMEM((BATCH * CAPACITY, width), jnp.bfloat16),
+            pltpu.VMEM((BATCH * CAPACITY, width), jnp.bfloat16),
             pltpu.VMEM(words, jnp.int32),
             pltpu.VMEM(words, jnp.int32),
             pltpu.VMEM((pairs, slots), jnp.bfloat16),

time: 46 us -> 42.7 us (0.928)
  Pallas kernels: 43.9 us -> 40.7 us
    pallas_call x1, Pallas kernels: 43.9 us -> 40.7 us  [fused(): pl.pallas_call(fused_kernel, out_shape=jax.ShapeDtypeStruct((pairs, list_...]
where the time goes in v3:
time: 42.7 us; the launch traced here: 42.6 us
  Pallas kernels  40.7 us (95%)
  local copies, waits for them, and re-layouts  1.87 us (4%)
    pallas_call x1, Pallas kernels, fused(): pl.pallas_call(fused_kernel, out_shape=jax.ShapeDtypeStruct((pairs, list_...  40.7 us
    unnamed x1, local copies, waits for them, and re-layouts  1.87 us

profile of v3, /device:TPU:0, one launch (start us, length us, event | category | flops | bytes accessed | tf_op | source)
XLA Modules:
  0.0 42.6 jit_solution(193185667601904284)
XLA Ops:
  0.0 40.7 %shard_map.55 = f32[512,256]{1,0:T(8,128)} custom-call(bf16[64,768]{1,0:T(8,128)(2,1)} %queries_hbm.1, bf16[768,768]{1,0:T(8,128)(2,1)} %projection_hbm.1, s32[8,64]{1,0:T(8,128)} %bitcast.4, s32[8,128]{1,0:T(8,128)} %bitcast.5, bf16[32,256,768]{2,1,0:T(8,128)(2,1)} %lists_hbm.1), custom_call_target="tpu_custom_call" | custom-call | tf_op jit(solution)/shard_map/pallas_call | solution.py:689
  40.7 1.9 %copy.7 = f32[64,8,256]{2,1,0:T(8,128)} copy(f32[64,8,256]{2,1,0:T(8,128)} %bitcast.3) | data formatting | bytes 1048576

commit v4 on v3

--- a/solution.py
+++ b/solution.py
@@ -353,10 +353,10 @@
         piece = pl.ds(n * part, part)
         return pltpu.make_async_copy(lists_hbm.at[piece], lists_ref.at[piece], list_sem.at[n])
 
+    for copy in inputs:
+        copy.wait()
     for n in range(list_sem.shape[0]):
         list_copy(n).start()
-    for copy in inputs:
-        copy.wait()
 
     projected = jnp.dot(
         queries_ref[...], projection_ref[...], preferred_element_type=jnp.float32
@@ -406,21 +406,24 @@
 
     send(me, *peers)
 
-    for n in range(list_sem.shape[0]):
-        list_copy(n).wait()
-        rows = []
-        for i in range(n * part, (n + 1) * part):
-            partial = None
-            for j in range(columns):
-                piece = lists_ref[i, :, j * LANES : (j + 1) * LANES].astype(jnp.float32)
-                partial = piece * piece if partial is None else partial + piece * piece
-            rows.append(0.5 * jnp.sum(partial.T, axis=0, keepdims=True))
-        norms_ref[n * part : (n + 1) * part, :] = jnp.concatenate(rows, axis=0)
-
-    relay(z, "a", sibling)
+    def list_norms(first, last):
+        for n in range(first, last):
+            list_copy(n).wait()
+            rows = []
+            for i in range(n * part, (n + 1) * part):
+                partial = None
+                for j in range(columns):
+                    piece = lists_ref[i, :, j * LANES : (j + 1) * LANES].astype(jnp.float32)
+                    partial = piece * piece if partial is None else partial + piece * piece
+                rows.append(0.5 * jnp.sum(partial.T, axis=0, keepdims=True))
+            norms_ref[n * part : (n + 1) * part, :] = jnp.concatenate(rows, axis=0)
+
+    list_norms(0, 5)
+    relay(z, "a", sibling, peer_b)
     relay(z, "b", sibling)
+    list_norms(5, 7)
     relay(cross, "o", peer_a, peer_b, sibling, peer_near)
-    send(peer_a, peer_b)
+    list_norms(7, 8)
 
     itself = (z, "o")
     batches = (
@@ -451,14 +454,14 @@
             (opposite, "x", True),
             (opposite, "y"),
             (opposite, "y", True),
-            (z, "d"),
             (near, "x"),
+            (near, "x", True),
         ),
         (
             (opposite, "d"),
             (opposite, "d", True),
+            (z, "d"),
             (z, "d", True),
-            (near, "x", True),
             (near, "y"),
             (near, "y", True),
             (near, "d"),
@@ -466,17 +469,6 @@
         ),
     )
     order = [block_of(*where).astype(jnp.float32) for chips in batches for where in chips]
-    target = jnp.where(lane8 < query_count, (stored >> 5).astype(jnp.float32), -1.0)
-    mine = jnp.concatenate([jnp.where(target == d, 1.0, 0.0) for d in order], axis=0)
-    rank = ranks(mine)
-    spot = jnp.zeros(ids.shape, jnp.float32)
-    for n, d in enumerate(order):
-        spot = jnp.where(target == d, rank[n * 8 : (n + 1) * 8] + float(n * capacity), spot)
-    wide = lax.broadcasted_iota(jnp.int32, (8, devices * capacity), 1).astype(jnp.float32)
-    for q in range(0, query_count, 2):
-        both = [jnp.where(spot[:, i : i + 1] == wide, 1.0, 0.0) for i in (q, q + 1)]
-        place_ref[q * 8 : (q + 2) * 8, :] = jnp.concatenate(both, axis=0).astype(jnp.bfloat16)
-
     def back(n):
         return pltpu.make_async_remote_copy(
             src_ref=send_ref.at[n],
@@ -563,10 +555,10 @@
             returned.append(copy)
 
     relays = {
+        (0, 2): ((opposite, "o", peer_a, peer_b, sibling),),
         (0, 3): (
             (cross, "a", peer_b, sibling),
             (cross, "b", sibling),
-            (opposite, "o", peer_a, peer_b, sibling),
             (z, "d", peer_near, sibling),
         ),
         (1, 2): (
@@ -632,6 +624,18 @@
         place, norm = later, after
     got_ref[0] = send_ref[0]
 
+    target = jnp.where(lane8 < query_count, (stored >> 5).astype(jnp.float32), -1.0)
+    mine = jnp.concatenate([jnp.where(target == d, 1.0, 0.0) for d in order], axis=0)
+    rank = ranks(mine)
+    spot = jnp.zeros(ids.shape, jnp.float32)
+    for n, d in enumerate(order):
+        spot = jnp.where(target == d, rank[n * 8 : (n + 1) * 8] + float(n * capacity), spot)
+    wide = lax.broadcasted_iota(jnp.int32, (8, devices * capacity), 1).astype(jnp.float32)
+    for q in range(0, query_count, 2):
+        both = [jnp.where(spot[:, i : i + 1] == wide, 1.0, 0.0) for i in (q, q + 1)]
+        place_ref[q * 8 : (q + 2) * 8, :] = jnp.concatenate(both, axis=0).astype(jnp.bfloat16)
+
+
     def receive(k):
         for copy in others(k):
             copy.wait_recv()
@@ -647,33 +651,41 @@
             [jnp.broadcast_to(powers[g : g + 1], (LANES, LANES)) for g in range(powers.shape[0])],
             axis=1,
         ).astype(jnp.bfloat16)
-        place = place_ref[:, k * slots : (k + count) * slots]
+        return codes, powers
+
+    def gather(codes, powers, rows, k):
+        place = place_ref[rows, k * slots : k * slots + codes.shape[0]]
         chosen = jnp.dot(place, codes, preferred_element_type=jnp.float32)
         power = lax.dot_general(
-            place,
-            powers,
-            (((1,), (1,)), ((), ())),
-            preferred_element_type=jnp.float32,
+            place, powers, (((1,), (1,)), ((), ())), preferred_element_type=jnp.float32
         )
         return jnp.concatenate([chosen, power], axis=1)
 
     for k in range(len(batches) - 1):
         receive(k)
-    total_ref[...] = unpack(0, len(batches) - 1)
-    receive(len(batches) - 1)
-    total = total_ref[...] + unpack(len(batches) - 1, 1)
-    scale = jnp.exp(total[:, 4 * LANES :] * LN2) * (1.0 / 65535.0)
-    for h in range(2):
-        low = total[:, 2 * h * LANES : (2 * h + 1) * LANES]
-        high = total[:, (2 * h + 1) * LANES : (2 * h + 2) * LANES]
-        out_ref[:, h * LANES : (h + 1) * LANES] = (low + 256.0 * high) * scale
-    result = pltpu.make_async_copy(out_ref, out_hbm, out_sem)
-    result.start()
+    final = len(batches) - 1
+    total_ref[...] = gather(*unpack(0, final), slice(None), 0)
+    receive(final)
+    unpacked = unpack(final, 1)
+    results = []
+    half = out_ref.shape[0] // 2
+    for n in range(2):
+        rows = slice(n * half, (n + 1) * half)
+        total = total_ref[rows, :] + gather(*unpacked, rows, final)
+        scale = jnp.exp(total[:, 4 * LANES :] * LN2) * (1.0 / 65535.0)
+        for h in range(2):
+            low = total[:, 2 * h * LANES : (2 * h + 1) * LANES]
+            high = total[:, (2 * h + 1) * LANES : (2 * h + 2) * LANES]
+            out_ref[rows, h * LANES : (h + 1) * LANES] = (low + 256.0 * high) * scale
+        part_of = pl.ds(n * half, half)
+        results.append(pltpu.make_async_copy(out_ref.at[part_of], out_hbm.at[part_of], out_sem.at[n]))
+        results[-1].start()
     for copy in sent:
         copy.wait_send()
     for copy in returned:
         copy.wait_send()
-    result.wait()
+    for copy in results:
+        copy.wait()
 
 
 def fused(queries, projection, lists, probes, owner_map):
@@ -712,7 +724,7 @@
             pltpu.SemaphoreType.DMA((devices,)),
             pltpu.SemaphoreType.DMA((devices,)),
             pltpu.SemaphoreType.DMA((devices,)),
-            pltpu.SemaphoreType.DMA,
+            pltpu.SemaphoreType.DMA((2,)),
         ],
         compiler_params=pltpu.CompilerParams(
             collective_id=0, has_side_effects=True, vmem_limit_bytes=VMEM_LIMIT

time: 42.7 us -> 41.8 us (0.979)
  Pallas kernels: 40.7 us -> 39.8 us
    pallas_call x1, Pallas kernels: 40.7 us -> 39.8 us  [fused(): pl.pallas_call(fused_kernel, out_shape=jax.ShapeDtypeStruct((pairs, list_...]
where the time goes in v4:
time: 41.8 us; the launch traced here: 41.7 us
  Pallas kernels  39.8 us (95%)
  local copies, waits for them, and re-layouts  1.87 us (4%)
    pallas_call x1, Pallas kernels, fused(): pl.pallas_call(fused_kernel, out_shape=jax.ShapeDtypeStruct((pairs, list_...  39.8 us
    unnamed x1, local copies, waits for them, and re-layouts  1.87 us

profile of v4, /device:TPU:0, one launch (start us, length us, event | category | flops | bytes accessed | tf_op | source)
XLA Modules:
  0.0 41.7 jit_solution(13988160438812307965)
XLA Ops:
  0.0 39.8 %shard_map.55 = f32[512,256]{1,0:T(8,128)} custom-call(bf16[64,768]{1,0:T(8,128)(2,1)} %queries_hbm.1, bf16[768,768]{1,0:T(8,128)(2,1)} %projection_hbm.1, s32[8,64]{1,0:T(8,128)} %bitcast.4, s32[8,128]{1,0:T(8,128)} %bitcast.5, bf16[32,256,768]{2,1,0:T(8,128)(2,1)} %lists_hbm.1), custom_call_target="tpu_custom_call" | custom-call | tf_op jit(solution)/shard_map/pallas_call | solution.py:701
  39.8 1.9 %copy.7 = f32[64,8,256]{2,1,0:T(8,128)} copy(f32[64,8,256]{2,1,0:T(8,128)} %bitcast.3) | data formatting | bytes 1048576

commit v5 on v4

--- a/solution.py
+++ b/solution.py
@@ -429,22 +429,22 @@
     batches = (
         (
             itself,
+            (z, "x"),
+            (z, "y"),
+            (cross, "o"),
             (z, "o", True),
-            (z, "x"),
             (z, "x", True),
-            (z, "y"),
             (z, "y", True),
-            (cross, "o"),
             (cross, "o", True),
         ),
         (
             (cross, "x"),
+            (cross, "y"),
+            (opposite, "o"),
+            (near, "o"),
             (cross, "x", True),
-            (cross, "y"),
             (cross, "y", True),
-            (opposite, "o"),
             (opposite, "o", True),
-            (near, "o"),
             (near, "o", True),
         ),
         (
@@ -495,7 +495,7 @@
         at = (rank, pltpu.roll(rank, query_count, 1))
         what = (pltpu.roll(local, query_count, 1), local)
         picks, lists_of = [], []
-        for t in range(BATCH):
+        for t in range(len(chips)):
             pick = jnp.zeros((capacity, LANES), jnp.float32)
             which = jnp.zeros((capacity, LANES), jnp.float32)
             for j in range(8):
@@ -506,8 +506,11 @@
             picks.append(pick.astype(jnp.bfloat16))
             lists_of.append(which)
         place = jnp.sum(jnp.concatenate(lists_of, axis=0), axis=1, keepdims=True)
-        place = jnp.broadcast_to(place, (slots, LANES))
+        place = jnp.broadcast_to(place, (place.shape[0], LANES))
         return picks, place
+
+    def join(one, two):
+        return one[0] + two[0], jnp.concatenate([one[1], two[1]], axis=0)
 
     def select(chips, picks, picked):
         norm = jnp.zeros((slots, LANES), jnp.float32)
@@ -549,8 +552,8 @@
     def others(k):
         return [back(n) for n in range(max(k * BATCH, 1), (k + 1) * BATCH)]
 
-    def give_back(k):
-        for copy in others(k):
+    def give_back(copies):
+        for copy in copies:
             copy.start()
             returned.append(copy)
 
@@ -568,15 +571,17 @@
             (near, "a", sibling),
             (near, "b", sibling),
         ),
-        (2, 1): ((near, "d", sibling), (opposite, "d", sibling)),
+        (2, 1): (
+            (near, "d", sibling),
+            (opposite, "d", sibling),
+        ),
     }
     picked_refs = (even_ref, odd_ref)
 
-    def prepare(k):
+    def complete(k):
         for where in batches[k]:
             if len(where) == 3:
                 arrived(block_of(*where))
-        return choose(batches[k])
 
     def score(k, place, best, first, count):
         dots = lax.dot_general(
@@ -594,11 +599,11 @@
         return best
 
     step = list_count // 4
-    for where in batches[0]:
-        if len(where) == 3:
-            arrived(block_of(*where))
-    relay(near, "o", peer_a, peer_b, sibling)
-    picks, place = choose(batches[0])
+    direct = BATCH // 2
+    early = choose(batches[0][:direct])
+    complete(0)
+    relay(near, "o", sibling, peer_a, peer_b)
+    picks, place = join(early, choose(batches[0][direct:]))
     norm = select(batches[0], picks, picked_refs[0])
     for k, chips in enumerate(batches):
         best = jnp.zeros((slots, list_size), jnp.float32)
@@ -612,15 +617,23 @@
                     relay(*item)
         ahead = 0 < k < len(batches) - 1
         if ahead:
-            picks, later = prepare(k + 1)
+            complete(k + 1)
+            picks, later = choose(batches[k + 1])
+        elif k == 0:
+            early = choose(batches[1][:direct])
         best = score(k, place, best, begin * step, (4 - begin) * step)
         if ahead:
             after = select(batches[k + 1], picks, picked_refs[(k + 1) % 2])
         encode(k, best, norm)
-        give_back(k)
         if k == 0:
-            picks, later = prepare(1)
+            give_back([back(direct - 1), back(BATCH - 1)])
+            complete(1)
+            picks, later = join(early, choose(batches[1][direct:]))
             after = select(batches[1], picks, picked_refs[1])
+        else:
+            give_back(others(k))
+        if k == 1:
+            give_back([back(n) for n in range(1, BATCH - 1) if n != direct - 1])
         place, norm = later, after
     got_ref[0] = send_ref[0]
 

time: 41.8 us -> 41.6 us (level)
  no operation moved by 1% of the time
where the time goes in v5:
time: 41.6 us; the launch traced here: 41.4 us
  Pallas kernels  39.6 us (95%)
  local copies, waits for them, and re-layouts  1.87 us (4%)
    pallas_call x1, Pallas kernels, fused(): pl.pallas_call(fused_kernel, out_shape=jax.ShapeDtypeStruct((pairs, list_...  39.6 us
    unnamed x1, local copies, waits for them, and re-layouts  1.87 us

profile of v5, /device:TPU:0, one launch (start us, length us, event | category | flops | bytes accessed | tf_op | source)
XLA Modules:
  0.0 41.4 jit_solution(10542745188359329202)
XLA Ops:
  0.0 39.6 %shard_map.55 = f32[512,256]{1,0:T(8,128)} custom-call(bf16[64,768]{1,0:T(8,128)(2,1)} %queries_hbm.1, bf16[768,768]{1,0:T(8,128)(2,1)} %projection_hbm.1, s32[8,64]{1,0:T(8,128)} %bitcast.4, s32[8,128]{1,0:T(8,128)} %bitcast.5, bf16[32,256,768]{2,1,0:T(8,128)(2,1)} %lists_hbm.1), custom_call_target="tpu_custom_call" | custom-call | tf_op jit(solution)/shard_map/pallas_call | solution.py:714
  39.6 1.9 %copy.7 = f32[64,8,256]{2,1,0:T(8,128)} copy(f32[64,8,256]{2,1,0:T(8,128)} %bitcast.3) | data formatting | bytes 1048576

commit v6 on v5

--- a/solution.py
+++ b/solution.py
@@ -565,16 +565,14 @@
             (z, "d", peer_near, sibling),
         ),
         (1, 2): (
-            (cross, "d", peer_near, sibling),
             (opposite, "a", sibling),
-            (opposite, "b", sibling),
             (near, "a", sibling),
             (near, "b", sibling),
+            (opposite, "b", sibling),
+            (cross, "d", peer_near, sibling),
         ),
-        (2, 1): (
-            (near, "d", sibling),
-            (opposite, "d", sibling),
-        ),
+        (2, 1): ((near, "d", sibling),),
+        (2, 2): ((opposite, "d", sibling),),
     }
     picked_refs = (even_ref, odd_ref)
 

time: 41.6 us -> 41.7 us (level)
  no operation moved by 1% of the time
where the time goes in v6:
time: 41.7 us; the launch traced here: 41.5 us
  Pallas kernels  39.6 us (95%)
  local copies, waits for them, and re-layouts  1.87 us (4%)
    pallas_call x1, Pallas kernels, fused(): pl.pallas_call(fused_kernel, out_shape=jax.ShapeDtypeStruct((pairs, list_...  39.6 us
    unnamed x1, local copies, waits for them, and re-layouts  1.87 us

profile of v6, /device:TPU:0, one launch (start us, length us, event | category | flops | bytes accessed | tf_op | source)
XLA Modules:
  0.0 41.5 jit_solution(12059869236289686375)
XLA Ops:
  0.0 39.6 %shard_map.55 = f32[512,256]{1,0:T(8,128)} custom-call(bf16[64,768]{1,0:T(8,128)(2,1)} %queries_hbm.1, bf16[768,768]{1,0:T(8,128)(2,1)} %projection_hbm.1, s32[8,64]{1,0:T(8,128)} %bitcast.4, s32[8,128]{1,0:T(8,128)} %bitcast.5, bf16[32,256,768]{2,1,0:T(8,128)(2,1)} %lists_hbm.1), custom_call_target="tpu_custom_call" | custom-call | tf_op jit(solution)/shard_map/pallas_call | solution.py:712
  39.6 1.9 %copy.7 = f32[64,8,256]{2,1,0:T(8,128)} copy(f32[64,8,256]{2,1,0:T(8,128)} %bitcast.3) | data formatting | bytes 1048576
